TPU v7x, 32 devices: a whole 2x2x4 slice. The times are simulated.
32 devices in a mesh: span: 4 (over y, x), leaf: 8 (over z, core).
Axes of the slice: x: 2, y: 2, z: 4, core: 2. Of those that a mesh axis runs over, the one named last changes fastest.
Arguments:
- populations: float32 [27, 64, 64, 128], P(None, 'span', 'leaf'), may hold values from 0.5 to 1.5
- relax_rates: float32 [27], replicated, may hold values from 1 to 1.6
- marker_forces: float32 [2, 3, 12288], P(None, None, ('span', 'leaf')), may hold values from -6 to 6
- marker_dest: int32 [2, 12288, 1], P(None, ('span', 'leaf')), may hold values from 0 to 7; in each aligned block of 384 rows (0 to 383, 384 to 767, ..., all dimensions but the last counted through in order) at most 144 rows name the same one
- marker_cells: int32 [2, 12288], P(None, ('span', 'leaf')), may hold values from 0 to 16383
Outputs:
- final_state: float32 [27, 64, 64, 128], P(None, 'span', 'leaf')
Inputs may be any that keep to these rules, and one draw needn't show every extreme that they name: `marker_dest`: in each step, no destination is named by more than 144 of the 384 markers of one device, and in every draw some device's markers name one destination exactly 144 times.
All inputs are finite; a program needn't handle non-finite values.
Results may differ from a plain program's by a relative error of at most 0.0001.
Values sent between devices are 32-bit elements; how exact they have to be, the bound alone decides.
A program may use at most 64 MiB of HBM per device.

v0:
```python
import jax
import jax.numpy as jnp
import numpy as np
from jax import lax
from jax.sharding import PartitionSpec as P

RHO_BASE = 27.0


def padded_2(block, sides, width):
    for axis, dim in sides:
        count = lax.axis_size(axis)
        forward = [(i, i + 1) for i in range(count - 1)]
        forward.append((count - 1, 0))
        backward = [(target, source) for source, target in forward]
        low = lax.ppermute(
            lax.slice_in_dim(block, block.shape[dim] - width, None, axis=dim), axis, forward
        )
        high = lax.ppermute(lax.slice_in_dim(block, 0, width, axis=dim), axis, backward)
        block = jnp.concatenate([low, block, high], axis=dim)
    return block


def lattice_tables():
    axis_values = np.array([-1.0, 0.0, 1.0])
    powers = np.array([[1.0, 1.0, 1.0], [-1.0, 0.0, 1.0], [1.0, 0.0, 1.0]])
    inverse = np.array([[0.0, -0.5, 0.5], [1.0, 0.0, -1.0], [0.0, 0.5, 0.5]])
    forward = np.kron(np.kron(powers, powers), powers)
    backward = np.kron(np.kron(inverse, inverse), inverse)
    one_weight = np.array([1.0 / 6.0, 2.0 / 3.0, 1.0 / 6.0])
    weights = np.kron(np.kron(one_weight, one_weight), one_weight)
    velocity = np.stack(
        np.meshgrid(axis_values, axis_values, axis_values, indexing="ij"), 0
    ).reshape(3, 27)
    return (forward, backward, weights, velocity)


def collide(populations, rates_cell, force_field, tables):
    forward = jnp.asarray(tables[0], dtype=jnp.float32)
    backward = jnp.asarray(tables[1], dtype=jnp.float32)
    weights = jnp.asarray(tables[2], dtype=jnp.float32)
    velocity = jnp.asarray(tables[3], dtype=jnp.float32)
    highest = lax.Precision.HIGHEST
    density = jnp.sum(populations, axis=0)
    momentum = jnp.einsum("dq,q...->d...", velocity, populations, precision=highest)
    velocity_field = momentum / RHO_BASE
    along = jnp.einsum("dq,d...->q...", velocity, velocity_field, precision=highest)
    square = jnp.sum(velocity_field * velocity_field, axis=0)
    shaped = weights.reshape((27,) + (1,) * (populations.ndim - 1))
    equilibrium = shaped * (density + RHO_BASE * (3.0 * along + 4.5 * along * along - 1.5 * square))
    moments = jnp.dot(forward, populations - equilibrium, precision=highest)
    relaxed = jnp.dot(backward, rates_cell * moments, precision=highest)
    source = 3.0 * shaped * jnp.einsum("dq,d...->q...", velocity, force_field, precision=highest)
    return populations - relaxed + source


def spread_forces(amounts, places, cell_count, width_y):
    highest = lax.Precision.HIGHEST
    outer_count = cell_count // width_y
    outer_ids = places // width_y
    inner_ids = places % width_y
    outer_hot = (outer_ids[:, None] == jnp.arange(outer_count, dtype=jnp.int32)[None, :]).astype(
        jnp.float32
    )
    inner_hot = (inner_ids[:, None] == jnp.arange(width_y, dtype=jnp.int32)[None, :]).astype(
        jnp.float32
    )
    weighted = amounts[:, :, None] * outer_hot[None, :, :]
    field = jnp.einsum("dso,sy->doy", weighted, inner_hot, precision=highest)
    return field.reshape(3, cell_count)


def deposit_forces(forces, destinations, cell_ids, cell_count, width_y):
    all_forces, all_ids = (
        lax.all_gather(forces, "leaf", axis=1, tiled=True),
        lax.all_gather(jnp.stack([destinations, cell_ids]), "leaf", axis=1, tiled=True),
    )
    occupied = all_ids[0] == lax.axis_index("leaf")
    places = jnp.where(occupied, all_ids[1], 0)
    amounts = jnp.where(occupied[None, :], all_forces, 0.0)
    return spread_forces(amounts, places, cell_count, width_y)


def stream_local(post, velocity):
    width_x = post.shape[1]
    width_z = post.shape[2]
    padded = padded_2(post, (("span", 1), ("leaf", 2)), 1)
    moved = []
    for direction in range(27):
        shift_x = int(velocity[0, direction])
        shift_y = int(velocity[1, direction])
        shift_z = int(velocity[2, direction])
        section = padded[
            direction, 1 - shift_x : 1 - shift_x + width_x, 1 - shift_z : 1 - shift_z + width_z
        ]
        moved.append(jnp.roll(section, shift_y, axis=2))
    return jnp.stack(moved)


def body(populations, relax_rates, marker_forces, marker_dest, marker_cells):
    tables = lattice_tables()
    width_x = populations.shape[1]
    width_z = populations.shape[2]
    width_y = populations.shape[3]
    cell_count = width_x * width_z * width_y
    rates_cell = relax_rates[:, None]
    state = populations.reshape(27, cell_count)
    for time_step in range(marker_forces.shape[0]):
        force_field = deposit_forces(
            marker_forces[time_step],
            marker_dest[time_step, :, 0],
            marker_cells[time_step],
            cell_count,
            width_y,
        )
        post = collide(state, rates_cell, force_field, tables)
        state = stream_local(post.reshape(27, width_x, width_z, width_y), tables[3]).reshape(
            27, cell_count
        )
    return state.reshape(27, width_x, width_z, width_y)


def solution(mesh):
    placed = (
        P(None, "span", "leaf", None),
        P(),
        P(None, None, ("span", "leaf")),
        P(None, ("span", "leaf"), None),
        P(None, ("span", "leaf")),
    )
    return jax.shard_map(
        body, mesh=mesh, in_specs=placed, out_specs=P(None, "span", "leaf", None), check_vma=False
    )
```

profile of v0, /device:TPU:0, one launch (start us, length us, event | category | flops | bytes accessed | tf_op | source)
XLA Modules:
  0.0 134.7 jit_solution(18437432149425876622)
XLA Ops:
  0.0 0.8 slice_bitcast_fusion.11
  0.8 0.8 fusion.108
  1.6 15.6 %all_gather.12 = s32[2,3072]{1,0:T(2,128)S(1)} all-gather(s32[2,384]{1,0:T(2,128)S(1)} %pad_add_fusion), channel_id=1, replica_groups=mesh['span'=4,'leaf'=8] {'leaf'}, dimensions={1}, use_global_device_ids=true | all-gather | bytes 27648 | tf_op jit(solution)/shard_map/all_gather | solution.py:76
  17.2 13.9 %all_gather.14 = s32[2,3072]{1,0:T(2,128)S(1)} all-gather(s32[2,384]{1,0:T(2,128)S(1)} %pad_add_fusion.1), channel_id=1, replica_groups=mesh['span'=4,'leaf'=8] {'leaf'}, dimensions={1}, use_global_device_ids=true | all-gather | bytes 27648 | tf_op jit(solution)/shard_map/all_gather | solution.py:76
  31.1 0.6 add_select_fusion.2
  31.9 0.8 fusion.107
  32.7 14.0 %all-gather = f32[1,3,3072]{2,1,0:T(4,128)S(1)} all-gather(f32[1,3,384]{2,1,0:T(4,128)S(1)} %copy.18), channel_id=2, replica_groups=mesh['span'=4,'leaf'=8] {'leaf'}, dimensions={2}, use_global_device_ids=true | all-gather | bytes 41472 | tf_op jit(solution)/shard_map/all_gather | solution.py:75
  46.8 0.3 pad.156
  47.1 1.2 copy.19
  48.3 1.2 multiply_reduce_fusion.1
  49.5 1.9 %fusion.109 = f32[27,16384]{1,0:T(8,128)S(1)} fusion(f32[3,27]{1,0:T(4,128)S(1)} %copy-done.7, f32[3,16384]{1,0:T(4,128)S(1)} %get-tuple-element.113), kind=kOutput, calls=%fused_computation.281 | convolution fusion | flops 15925248 | bytes 1966404 | tf_op jit(solution)/shard_map/dq,d...->q.../dot_general | solution.py:47
  51.5 2.8 %convolution_multiply_fusion.3 = f32[16384,27]{0,1:T(8,128)S(1)} fusion(f32[27,27]{1,0:T(8,128)S(1)} %copy-done.6, f32[27,16384]{1,0:T(8,128)S(1)} %bitcast.382, f32[27,16384]{1,0:T(8,128)S(1)} %fusion.109, f32[16384]{0:T(1024)S(1)} %broadcast_multiply_fusion.2, f32[16384]{0:T(1024)S(1)} %bitcast.483, f32[27]{0:T(128)S(1)} %copy-done.12, f32[27]{0:T(128)S(1)} %copy-done.11), kind=kOutput, calls=%fused_computation.9 | convolution fusion | flops 147308544 | bytes 5442620 | tf_op jit(solution)/shard_map/dot_general | solution.py:51
  54.4 1.9 %convolution_subtract_fusion.1 = f32[27,16384]{1,0:T(8,128)S(1)} fusion(f32[27,16384]{1,0:T(8,128)S(1)} %bitcast.383, f32[27,27]{1,0:T(8,128)S(1)} %copy-done.5, f32[16384,27]{0,1:T(8,128)S(1)} %convolution_multiply_fusion.3), kind=kOutput, calls=%fused_computation.8 | convolution fusion | flops 143769600 | bytes 5311332 | tf_op jit(solution)/shard_map/dot_general | solution.py:52
  56.3 2.6 %fusion.32 = f32[1,3,128,128]{3,2,1,0:T(8,128)S(1)} fusion(f32[3072,128]{0,1:T(8,128)S(1)} %fusion.26, f32[3,3072]{1,0:T(4,128)S(1)} %bitcast_select_fusion.1, s32[3072]{0:T(1024)S(1)} %copy-done.8), kind=kOutput, calls=%fused_computation.43 | convolution fusion | flops 1813512192 | bytes 1818624 | tf_op jit(solution)/shard_map/dso,sy->doy/dot_general | solution.py:69
  58.9 2.1 %fusion.3 = f32[27,16384]{1,0:T(8,128)S(1)} fusion(f32[27,16384]{1,0:T(8,128)S(1)} %convolution_subtract_fusion.1, f32[3,27]{1,0:T(4,128)S(1)} %copy-done.7, f32[27]{0:T(128)S(1)} %copy-done.10, f32[1,3,128,128]{3,2,1,0:T(8,128)S(1)} %fusion.32), kind=kOutput, calls=%fused_computation.7 | convolution fusion | flops 16809984 | bytes 3735984 | tf_op jit(solution)/shard_map/dq,d...->q.../dot_general | solution.py:53
  61.1 0.4 copy.21
  61.6 1.5 %collective-permute-start = (f32[27,1,8,128]{3,2,1,0:T(8,128)S(1)}, f32[27,1,8,128]{3,2,1,0:T(8,128)S(1)}, u32[]{:S(2)}, u32[]{:S(2)}) collective-permute-start(f32[27,1,8,128]{3,2,1,0:T(8,128)S(1)} %get-tuple-element.93), channel_id=1, source_target_pairs={{0,8},{8,16},{16,24},{24,0},{1,9},{9,17},{17,25},{25,1},{2,10},{10... | collective-permute-start | bytes 331784 | tf_op jit(solution)/shard_map/ppermute | solution.py:16
  63.1 1.4 %collective-permute-start.1 = (f32[27,1,8,128]{3,2,1,0:T(8,128)S(1)}, f32[27,1,8,128]{3,2,1,0:T(8,128)S(1)}, u32[]{:S(2)}, u32[]{:S(2)}) collective-permute-start(f32[27,1,8,128]{3,2,1,0:T(8,128)S(1)} %get-tuple-element.92), channel_id=1, source_target_pairs={{8,0},{16,8},{24,16},{0,24},{9,1},{17,9},{25,17},{1,25},{10,2},{18... | collective-permute-start | bytes 331784 | tf_op jit(solution)/shard_map/ppermute | solution.py:19
  65.0 12.7 %all-gather.1 = f32[1,3,3072]{2,0,1:T(1,128)S(1)} all-gather(f32[1,3,384]{2,0,1:T(1,128)S(1)} %get-tuple-element.107), channel_id=3, replica_groups=mesh['span'=4,'leaf'=8] {'leaf'}, dimensions={2}, use_global_device_ids=true | all-gather | bytes 41472 | tf_op jit(solution)/shard_map/all_gather | solution.py:75
  77.7 2.6 %fusion.37 = f32[1,3,128,128]{3,2,1,0:T(8,128)S(1)} fusion(f32[3072,128]{0,1:T(8,128)S(1)} %fusion.29, f32[3,3072]{1,0:T(4,128)S(1)} %bitcast_select_fusion, s32[3072]{0:T(1024)S(1)} %get-tuple-element.104), kind=kOutput, calls=%fused_computation.44 | convolution fusion | flops 1813512192 | bytes 1818624 | tf_op jit(solution)/shard_map/dso,sy->doy/dot_general | solution.py:69
  80.3 3.2 %fusion = f32[27,16384]{1,0:T(8,128)} fusion(f32[3,27]{1,0:T(4,128)S(1)} %copy-done.7, f32[27]{0:T(128)S(1)} %copy-done.10, f32[1,3,128,128]{3,2,1,0:T(8,128)S(1)} %fusion.37), kind=kOutput, calls=%fused_computation.1 | convolution fusion | flops 16367616 | bytes 1966512 | tf_op jit(solution)/shard_map/dq,d...->q.../dot_general | solution.py:53
  83.7 0.4 constant_dynamic-update-slice_fusion.1
  84.1 0.3 fusion.104
  84.4 1.9 %collective-permute-start.2 = (f32[27,18,1,128]{3,2,1,0:T(1,128)S(1)}, f32[27,18,1,128]{3,2,1,0:T(1,128)S(1)}, u32[]{:S(2)}, u32[]{:S(2)}) collective-permute-start(f32[27,18,1,128]{3,2,1,0:T(1,128)S(1)} %get-tuple-element.76), channel_id=1, source_target_pairs={{1,0},{2,1},{3,2},{4,3},{5,4},{6,5},{7,6},{0,7},{9,8},{10,9},{11,1... | collective-permute-start | bytes 746504 | tf_op jit(solution)/shard_map/ppermute | solution.py:19
  86.4 0.6 slice_bitcast_fusion.13
  87.0 0.6 slice_bitcast_fusion.12
  88.0 4.3 %collective-permute-done.2 = f32[27,18,1,128]{3,2,1,0:T(1,128)S(1)} collective-permute-done((f32[27,18,1,128]{3,2,1,0:T(1,128)S(1)}, f32[27,18,1,128]{3,2,1,0:T(1,128)S(1)}, u32[]{:S(2)}, u32[]{:S(2)}) %collective-permute-start.2) | collective-permute-done | bytes 248864 | tf_op jit(solution)/shard_map/ppermute | solution.py:19
  92.9 1.0 collective-permute-done.3
  94.8 1.3 fusion.89
  96.3 1.4 %multiply_reduce_fusion = (f32[16384]{0:T(1024)S(1)}, f32[16384,3]{0,1:T(4,128)S(1)}) fusion(f32[16384]{0:T(1024)S(1)} %bitcast.394, f32[3]{0:T(128)S(1)} %copy-done.24, f32[16384]{0:T(1024)S(1)} %bitcast.396, f32[3]{0:T(128)S(1)} %copy-done.23, f32[16384]{0:T(1024)S(1)} %bitcast.398, f32[3]{0:T(128)S(1)} %copy-done.22, f32[16384]{0:T(1024)S(1)} %bitcast.400, ...), kind=kLoop, calls=%fused_computation.90 | loop fusion | flops 2588672 | bytes 2031904 | tf_op jit(solution)/shard_map/reduce_sum | solution.py:48
  97.7 3.2 %fusion.110 = f32[27,16384]{1,0:T(8,128)} fusion(f32[3,27]{1,0:T(4,128)S(1)} %copy-done.7, f32[16384,3]{0,1:T(4,128)S(1)} %get-tuple-element.31), kind=kOutput, calls=%fused_computation.282 | convolution fusion | flops 15925248 | bytes 1966404 | tf_op jit(solution)/shard_map/dq,d...->q.../dot_general | solution.py:47
  100.9 0.6 broadcast_multiply_fusion.1
  101.6 4.3 %stack.181 = f32[27,16384]{1,0:T(8,128)S(1)} concatenate(f32[1,16384]{1,0:T(1,128)} %bitcast.440, f32[1,16384]{1,0:T(1,128)} %bitcast.439, f32[1,16384]{1,0:T(1,128)} %bitcast.437, f32[1,16384]{1,0:T(1,128)S(1)} %bitcast.435, f32[1,16384]{1,0:T(1,128)} %bitcast.481, f32[1,16384]{1,0:T(1,128)S(1)} %bitcast.433, f32[1,16384]{1,0:T(1,128)S(1)} %bitcast.431, ...), dimensions={0} | concatenate | bytes 3538944 | tf_op jit(solution)/shard_map/stack | solution.py:97
  105.9 4.6 %convolution_multiply_fusion.1 = f32[16384,27]{0,1:T(8,128)S(1)} fusion(f32[27,27]{1,0:T(8,128)} %constant.68.clone, f32[27,16384]{1,0:T(8,128)S(1)} %stack.181, f32[27,16384]{1,0:T(8,128)} %fusion.110, f32[16384]{0:T(1024)} %broadcast_multiply_fusion.1, f32[16384]{0:T(1024)} %get-tuple-element.5, f32[27]{0:T(128)} %constant.70.clone, f32[27]{0:T(128)} %param.14), kind=kOutput, calls=%fused_computation.4 | convolution fusion | flops 147308544 | bytes 5442620 | tf_op jit(solution)/shard_map/dot_general | solution.py:51
  110.5 2.1 %fusion.1 = f32[27,16384]{1,0:T(8,128)S(1)} fusion(f32[27,16384]{1,0:T(8,128)S(1)} %copy-done, f32[27,16384]{1,0:T(8,128)S(1)} %stack.181, f32[27,27]{1,0:T(8,128)S(1)} %copy-done.5, f32[16384,27]{0,1:T(8,128)S(1)} %convolution_multiply_fusion.1), kind=kOutput, calls=%fused_computation.3 | convolution fusion | flops 144211968 | bytes 7080804 | tf_op jit(solution)/shard_map/dot_general | solution.py:52
  112.6 0.4 copy.23
  113.0 0.2 slice_bitcast_fusion
  113.2 0.6 collective-permute-start.4
  114.0 2.4 %collective-permute-start.5 = (f32[27,1,8,128]{3,2,1,0:T(8,128)S(1)}, f32[27,1,8,128]{3,2,1,0:T(8,128)S(1)}, u32[]{:S(2)}, u32[]{:S(2)}) collective-permute-start(f32[27,1,8,128]{3,2,1,0:T(8,128)S(1)} %get-tuple-element.90), channel_id=1, source_target_pairs={{8,0},{16,8},{24,16},{0,24},{9,1},{17,9},{25,17},{1,25},{10,2},{18... | collective-permute-start | bytes 331784 | tf_op jit(solution)/shard_map/ppermute | solution.py:19
  116.5 2.4 %collective-permute-done.4 = f32[27,1,8,128]{3,2,1,0:T(8,128)S(1)} collective-permute-done((f32[27,1,8,128]{3,2,1,0:T(8,128)S(1)}, f32[27,1,8,128]{3,2,1,0:T(8,128)S(1)}, u32[]{:S(2)}, u32[]{:S(2)}) %collective-permute-start.4) | collective-permute-done | bytes 110624 | tf_op jit(solution)/shard_map/ppermute | solution.py:16
  118.9 0.3 constant_dynamic-update-slice_fusion.12
  119.3 0.9 collective-permute-done.5
  120.2 0.3 fusion.103
  120.5 1.6 %collective-permute-start.6 = (f32[27,18,1,128]{3,2,1,0:T(1,128)S(1)}, f32[27,18,1,128]{3,2,1,0:T(1,128)S(1)}, u32[]{:S(2)}, u32[]{:S(2)}) collective-permute-start(f32[27,18,1,128]{3,2,1,0:T(1,128)S(1)} %get-tuple-element.75), channel_id=1, source_target_pairs={{1,0},{2,1},{3,2},{4,3},{5,4},{6,5},{7,6},{0,7},{9,8},{10,9},{11,1... | collective-permute-start | bytes 746504 | tf_op jit(solution)/shard_map/ppermute | solution.py:19
  122.2 5.7 %collective-permute-done.6 = f32[27,18,1,128]{3,2,1,0:T(1,128)S(1)} collective-permute-done((f32[27,18,1,128]{3,2,1,0:T(1,128)S(1)}, f32[27,18,1,128]{3,2,1,0:T(1,128)S(1)}, u32[]{:S(2)}, u32[]{:S(2)}) %collective-permute-start.6) | collective-permute-done | bytes 248864 | tf_op jit(solution)/shard_map/ppermute | solution.py:19
  128.0 1.7 %collective-permute-done.7 = f32[27,18,1,128]{3,2,1,0:T(1,128)S(1)} collective-permute-done((f32[27,18,1,128]{3,2,1,0:T(1,128)S(1)}, f32[27,18,1,128]{3,2,1,0:T(1,128)S(1)}, u32[]{:S(2)}, u32[]{:S(2)}) %collective-permute-start.7) | collective-permute-done | bytes 248864 | tf_op jit(solution)/shard_map/ppermute | solution.py:16
  132.8 1.2 copy-done.9
  134.0 0.7 constant_dynamic-update-slice_fusion.14
  (168 shorter events, 6.2 us)
Async XLA Ops:
  0.0 46.7 %copy-start.1 = (f32[27,16,8,128]{3,2,1,0:T(8,128)S(1)}, f32[27,16,8,128]{3,2,1,0:T(8,128)}, u32[]{:S(2)}) copy-start(f32[27,16,8,128]{3,2,1,0:T(8,128)} %param.13) | copy-start | bytes 5308420
  47.1 1.2 copy-start.7
  49.5 2.0 %copy-start.6 = (f32[27,27]{1,0:T(8,128)S(1)}, f32[27,27]{1,0:T(8,128)}, u32[]{:S(2)}) copy-start(f32[27,27]{1,0:T(8,128)} %constant.68.clone) | copy-start | bytes 8752
  49.5 2.0 %copy-start.11 = (f32[27]{0:T(128)S(1)}, f32[27]{0:T(128)}, u32[]{:S(2)}) copy-start(f32[27]{0:T(128)} %param.14) | copy-start | bytes 328
  49.5 2.0 %copy-start.12 = (f32[27]{0:T(128)S(1)}, f32[27]{0:T(128)}, u32[]{:S(2)}) copy-start(f32[27]{0:T(128)} %constant.70.clone) | copy-start | bytes 328
  51.5 2.8 %copy-start.5 = (f32[27,27]{1,0:T(8,128)S(1)}, f32[27,27]{1,0:T(8,128)}, u32[]{:S(2)}) copy-start(f32[27,27]{1,0:T(8,128)} %constant.69.clone) | copy-start | bytes 8752
  54.3 2.0 %copy-start.8 = (s32[3072]{0:T(1024)S(1)}, s32[3072]{0:T(1024)}, u32[]{:S(2)}) copy-start(s32[3072]{0:T(1024)} %get-tuple-element.102) | copy-start | bytes 36868
  56.3 2.6 %copy-start.10 = (f32[27]{0:T(128)S(1)}, f32[27]{0:T(128)}, u32[]{:S(2)}) copy-start(f32[27]{0:T(128)} %constant.72) | copy-start | bytes 328
  61.6 22.1 %collective-permute-start = (f32[27,1,8,128]{3,2,1,0:T(8,128)S(1)}, f32[27,1,8,128]{3,2,1,0:T(8,128)S(1)}, u32[]{:S(2)}, u32[]{:S(2)}) collective-permute-start(f32[27,1,8,128]{3,2,1,0:T(8,128)S(1)} %get-tuple-element.93), channel_id=1, source_target_pairs={{0,8},{8,16},{16,24},{24,0},{1,9},{9,17},{17,25},{25,1},{2,10},{10... | collective-permute-start | bytes 331784 | tf_op jit(solution)/shard_map/ppermute | solution.py:16
  63.1 20.9 %collective-permute-start.1 = (f32[27,1,8,128]{3,2,1,0:T(8,128)S(1)}, f32[27,1,8,128]{3,2,1,0:T(8,128)S(1)}, u32[]{:S(2)}, u32[]{:S(2)}) collective-permute-start(f32[27,1,8,128]{3,2,1,0:T(8,128)S(1)} %get-tuple-element.92), channel_id=1, source_target_pairs={{8,0},{16,8},{24,16},{0,24},{9,1},{17,9},{25,17},{1,25},{10,2},{18... | collective-permute-start | bytes 331784 | tf_op jit(solution)/shard_map/ppermute | solution.py:19
  84.4 7.9 %collective-permute-start.2 = (f32[27,18,1,128]{3,2,1,0:T(1,128)S(1)}, f32[27,18,1,128]{3,2,1,0:T(1,128)S(1)}, u32[]{:S(2)}, u32[]{:S(2)}) collective-permute-start(f32[27,18,1,128]{3,2,1,0:T(1,128)S(1)} %get-tuple-element.76), channel_id=1, source_target_pairs={{1,0},{2,1},{3,2},{4,3},{5,4},{6,5},{7,6},{0,7},{9,8},{10,9},{11,1... | collective-permute-start | bytes 746504 | tf_op jit(solution)/shard_map/ppermute | solution.py:19
  86.4 7.6 %collective-permute-start.3 = (f32[27,18,1,128]{3,2,1,0:T(1,128)S(1)}, f32[27,18,1,128]{3,2,1,0:T(1,128)S(1)}, u32[]{:S(2)}, u32[]{:S(2)}) collective-permute-start(f32[27,18,1,128]{3,2,1,0:T(1,128)S(1)} %get-tuple-element.77), channel_id=1, source_target_pairs={{0,1},{1,2},{2,3},{3,4},{4,5},{5,6},{6,7},{7,0},{8,9},{9,10},{10,1... | collective-permute-start | bytes 746504 | tf_op jit(solution)/shard_map/ppermute | solution.py:16
  94.5 1.6 %copy-start.13 = (f32[3]{0:T(128)S(1)}, f32[3]{0:T(128)}, u32[]{:S(2)}) copy-start(f32[3]{0:T(128)} %constant.102) | copy-start | bytes 40
  94.5 1.6 %copy-start.14 = (f32[3]{0:T(128)S(1)}, f32[3]{0:T(128)}, u32[]{:S(2)}) copy-start(f32[3]{0:T(128)} %constant.104) | copy-start | bytes 40
  94.5 1.6 %copy-start.15 = (f32[3]{0:T(128)S(1)}, f32[3]{0:T(128)}, u32[]{:S(2)}) copy-start(f32[3]{0:T(128)} %constant.106) | copy-start | bytes 40
  94.5 1.6 %copy-start.16 = (f32[3]{0:T(128)S(1)}, f32[3]{0:T(128)}, u32[]{:S(2)}) copy-start(f32[3]{0:T(128)} %constant.108) | copy-start | bytes 40
  94.5 1.6 %copy-start.17 = (f32[3]{0:T(128)S(1)}, f32[3]{0:T(128)}, u32[]{:S(2)}) copy-start(f32[3]{0:T(128)} %constant.110) | copy-start | bytes 40
  94.6 1.6 %copy-start.18 = (f32[3]{0:T(128)S(1)}, f32[3]{0:T(128)}, u32[]{:S(2)}) copy-start(f32[3]{0:T(128)} %constant.112) | copy-start | bytes 40
  94.6 1.6 %copy-start.19 = (f32[3]{0:T(128)S(1)}, f32[3]{0:T(128)}, u32[]{:S(2)}) copy-start(f32[3]{0:T(128)} %constant.114) | copy-start | bytes 40
  94.6 1.6 %copy-start.20 = (f32[3]{0:T(128)S(1)}, f32[3]{0:T(128)}, u32[]{:S(2)}) copy-start(f32[3]{0:T(128)} %constant.116) | copy-start | bytes 40
  94.6 1.6 %copy-start.21 = (f32[3]{0:T(128)S(1)}, f32[3]{0:T(128)}, u32[]{:S(2)}) copy-start(f32[3]{0:T(128)} %constant.118) | copy-start | bytes 40
  94.6 1.6 %copy-start.22 = (f32[3]{0:T(128)S(1)}, f32[3]{0:T(128)}, u32[]{:S(2)}) copy-start(f32[3]{0:T(128)} %constant.120) | copy-start | bytes 40
  94.6 1.5 %copy-start.23 = (f32[3]{0:T(128)S(1)}, f32[3]{0:T(128)}, u32[]{:S(2)}) copy-start(f32[3]{0:T(128)} %constant.122) | copy-start | bytes 40
  94.6 1.5 %copy-start.24 = (f32[3]{0:T(128)S(1)}, f32[3]{0:T(128)}, u32[]{:S(2)}) copy-start(f32[3]{0:T(128)} %constant.124) | copy-start | bytes 40
  94.7 1.5 %copy-start.25 = (f32[3]{0:T(128)S(1)}, f32[3]{0:T(128)}, u32[]{:S(2)}) copy-start(f32[3]{0:T(128)} %constant.76) | copy-start | bytes 40
  94.7 1.5 %copy-start.26 = (f32[3]{0:T(128)S(1)}, f32[3]{0:T(128)}, u32[]{:S(2)}) copy-start(f32[3]{0:T(128)} %constant.78) | copy-start | bytes 40
  94.7 1.5 %copy-start.27 = (f32[3]{0:T(128)S(1)}, f32[3]{0:T(128)}, u32[]{:S(2)}) copy-start(f32[3]{0:T(128)} %constant.80) | copy-start | bytes 40
  94.7 1.5 %copy-start.28 = (f32[3]{0:T(128)S(1)}, f32[3]{0:T(128)}, u32[]{:S(2)}) copy-start(f32[3]{0:T(128)} %constant.82) | copy-start | bytes 40
  94.7 1.5 %copy-start.29 = (f32[3]{0:T(128)S(1)}, f32[3]{0:T(128)}, u32[]{:S(2)}) copy-start(f32[3]{0:T(128)} %constant.84) | copy-start | bytes 40
  94.7 1.5 %copy-start.30 = (f32[3]{0:T(128)S(1)}, f32[3]{0:T(128)}, u32[]{:S(2)}) copy-start(f32[3]{0:T(128)} %constant.86) | copy-start | bytes 40
  94.7 1.5 %copy-start.31 = (f32[3]{0:T(128)S(1)}, f32[3]{0:T(128)}, u32[]{:S(2)}) copy-start(f32[3]{0:T(128)} %constant.88) | copy-start | bytes 40
  94.7 1.5 %copy-start.32 = (f32[3]{0:T(128)S(1)}, f32[3]{0:T(128)}, u32[]{:S(2)}) copy-start(f32[3]{0:T(128)} %constant.90) | copy-start | bytes 40
  94.8 1.5 %copy-start.33 = (f32[3]{0:T(128)S(1)}, f32[3]{0:T(128)}, u32[]{:S(2)}) copy-start(f32[3]{0:T(128)} %constant.92) | copy-start | bytes 40
  94.8 1.5 %copy-start.34 = (f32[3]{0:T(128)S(1)}, f32[3]{0:T(128)}, u32[]{:S(2)}) copy-start(f32[3]{0:T(128)} %constant.94) | copy-start | bytes 40
  94.8 1.5 %copy-start.35 = (f32[3]{0:T(128)S(1)}, f32[3]{0:T(128)}, u32[]{:S(2)}) copy-start(f32[3]{0:T(128)} %constant.96) | copy-start | bytes 40
  94.8 1.5 %copy-start.36 = (f32[3]{0:T(128)S(1)}, f32[3]{0:T(128)}, u32[]{:S(2)}) copy-start(f32[3]{0:T(128)} %constant.98) | copy-start | bytes 40
  96.1 4.9 %copy-start.2 = (f32[16,8,128]{2,1,0:T(8,128)}, f32[16,8,128]{2,1,0:T(8,128)S(1)}, u32[]{:S(2)}) copy-start(f32[16,8,128]{2,1,0:T(8,128)S(1)} %get-tuple-element.27) | copy-start | bytes 196612
  96.1 4.9 %copy-start.3 = (f32[16,8,128]{2,1,0:T(8,128)}, f32[16,8,128]{2,1,0:T(8,128)S(1)}, u32[]{:S(2)}) copy-start(f32[16,8,128]{2,1,0:T(8,128)S(1)} %get-tuple-element.28) | copy-start | bytes 196612
  96.1 4.9 %copy-start.4 = (f32[16,8,128]{2,1,0:T(8,128)}, f32[16,8,128]{2,1,0:T(8,128)S(1)}, u32[]{:S(2)}) copy-start(f32[16,8,128]{2,1,0:T(8,128)S(1)} %get-tuple-element.29) | copy-start | bytes 196612
  105.9 4.6 %copy-start = (f32[27,16384]{1,0:T(8,128)S(1)}, f32[27,16384]{1,0:T(8,128)}, u32[]{:S(2)}) copy-start(f32[27,16384]{1,0:T(8,128)} %fusion) | copy-start | bytes 5308420
  113.2 5.7 %collective-permute-start.4 = (f32[27,1,8,128]{3,2,1,0:T(8,128)S(1)}, f32[27,1,8,128]{3,2,1,0:T(8,128)S(1)}, u32[]{:S(2)}, u32[]{:S(2)}) collective-permute-start(f32[27,1,8,128]{3,2,1,0:T(8,128)S(1)} %get-tuple-element.91), channel_id=1, source_target_pairs={{0,8},{8,16},{16,24},{24,0},{1,9},{9,17},{17,25},{25,1},{2,10},{10... | collective-permute-start | bytes 331784 | tf_op jit(solution)/shard_map/ppermute | solution.py:16
  114.0 6.2 %collective-permute-start.5 = (f32[27,1,8,128]{3,2,1,0:T(8,128)S(1)}, f32[27,1,8,128]{3,2,1,0:T(8,128)S(1)}, u32[]{:S(2)}, u32[]{:S(2)}) collective-permute-start(f32[27,1,8,128]{3,2,1,0:T(8,128)S(1)} %get-tuple-element.90), channel_id=1, source_target_pairs={{8,0},{16,8},{24,16},{0,24},{9,1},{17,9},{25,17},{1,25},{10,2},{18... | collective-permute-start | bytes 331784 | tf_op jit(solution)/shard_map/ppermute | solution.py:19
  120.5 7.5 %collective-permute-start.6 = (f32[27,18,1,128]{3,2,1,0:T(1,128)S(1)}, f32[27,18,1,128]{3,2,1,0:T(1,128)S(1)}, u32[]{:S(2)}, u32[]{:S(2)}) collective-permute-start(f32[27,18,1,128]{3,2,1,0:T(1,128)S(1)} %get-tuple-element.75), channel_id=1, source_target_pairs={{1,0},{2,1},{3,2},{4,3},{5,4},{6,5},{7,6},{0,7},{9,8},{10,9},{11,1... | collective-permute-start | bytes 746504 | tf_op jit(solution)/shard_map/ppermute | solution.py:19
  122.1 7.6 %collective-permute-start.7 = (f32[27,18,1,128]{3,2,1,0:T(1,128)S(1)}, f32[27,18,1,128]{3,2,1,0:T(1,128)S(1)}, u32[]{:S(2)}, u32[]{:S(2)}) collective-permute-start(f32[27,18,1,128]{3,2,1,0:T(1,128)S(1)} %get-tuple-element.74), channel_id=1, source_target_pairs={{0,1},{1,2},{2,3},{3,4},{4,5},{5,6},{6,7},{7,0},{8,9},{9,10},{10,1... | collective-permute-start | bytes 746504 | tf_op jit(solution)/shard_map/ppermute | solution.py:16
  132.7 1.2 copy-start.9
where the time goes:
time: 135 us
  blocking collectives  56.1 us (42%)
  matrix products  28.3 us (21%)
  local copies, waits for them, and re-layouts  16.6 us (12%)
  waiting for transfers between devices  16 us (12%)
  starting transfers between devices  9.54 us (7%)
  other arithmetic  7.11 us (5%)
    all_gather x2, blocking collectives, deposit_forces(): lax.all_gather(jnp.stack([destinations, cell_ids]), 'leaf', axis=1, tiled...  29.4 us
    all_gather x2, blocking collectives, deposit_forces(): lax.all_gather(forces, 'leaf', axis=1, tiled=True)  26.7 us
    ppermute x4, waiting for transfers between devices, padded_2(): lax.ppermute(lax.slice_in_dim(block, 0, width, axis=dim), axis, backward)  10.9 us
    dot_general x2, matrix products, collide(): moments = jnp.dot(forward, populations - equilibrium, precision=highest)  7.4 us
    ppermute x4, starting transfers between devices, padded_2(): lax.ppermute(lax.slice_in_dim(block, 0, width, axis=dim), axis, backward)  7.36 us
    dot_general x2, matrix products, collide(): jnp.einsum('dq,d...->q...', velocity, force_field, precision=highest)  5.33 us
    dot_general x2, matrix products, spread_forces(): field = jnp.einsum('dso,sy->doy', weighted, inner_hot, precision=highest)  5.22 us
    ppermute x4, waiting for transfers between devices, padded_2(): lax.ppermute(lax.slice_in_dim(block, block.shape[dim] - width, None, axis...  5.13 us
  transfers between devices with their start and end apart: 8, of which 6 were waited for; matrix products, arithmetic and copies ran while one was open for 7% of the time, Pallas kernels for 0%

commit v1 on v0

v1 whole, which is shorter than its diff:
```python
import functools

import jax
import jax.numpy as jnp
from jax import lax
from jax.experimental import pallas as pl
from jax.experimental.pallas import tpu as pltpu
from jax.sharding import PartitionSpec as P

MESH = pl.DeviceIdType.MESH
F32 = jnp.float32
BF16 = jnp.bfloat16


def parts(index):
    return index // 9, (index // 3) % 3, index % 3


def forward(values):
    for stride in (1, 3, 9):
        moved = list(values)
        for low in range(27):
            if (low // stride) % 3 == 0:
                a, b, c = (values[low + stride * i] for i in range(3))
                both = a + c
                moved[low] = both + b
                moved[low + stride] = c - a
                moved[low + 2 * stride] = both
        values = moved
    return values


def backward(values):
    for stride in (9, 3, 1):
        moved = list(values)
        for low in range(27):
            if (low // stride) % 3 == 0:
                a, b, c = (values[low + stride * i] for i in range(3))
                moved[low] = c - b
                moved[low + stride] = a - (c + c)
                moved[low + 2 * stride] = c + b
        values = moved
    return values


def relax(m, keep, pull):
    momentum = (m[9], m[3], m[1])
    squares = [v * v * (1.0 / 9.0) for v in momentum]
    result = []
    for k in range(27):
        power = parts(k)
        ones = [i for i in range(3) if power[i] == 1]
        if len(ones) == 3:
            result.append(keep(k) * m[k])
            continue
        if len(ones) == 2:
            target = momentum[ones[0]] * momentum[ones[1]] * (1.0 / 27.0)
        elif len(ones) == 1:
            target = momentum[ones[0]]
        else:
            target = m[0]
            for i in range(3):
                if power[i] == 2:
                    target = target + squares[i]
        result.append(keep(k) * m[k] + pull(k) * target)
    return result


def add_force(n, force):
    n = list(n)
    for k in range(27):
        power = parts(k)
        ones = [i for i in range(3) if power[i] == 1]
        if len(ones) == 1:
            twos = sum(1 for p in power if p == 2)
            factor = 0.5 * (0.5 / 3.0) ** twos
            n[k] = n[k] + factor * force[ones[0]]
    return n


def kernel(
    spans, leaves,
    pop, rates, forces, dest, cells, out,
    f, pa, pb, coef, force, hot_a, hot_b,
    m_forces, m_dest, m_cells, m_send, m_recv,
    send_p, send_m, zlo, zhi,
    in_sem, out_sem, ms_sem, mr_sem, hs_sem, hr_sem,
):
    wx = pop.shape[1]
    count = cells.shape[1]
    me_s = lax.axis_index("span")
    me_l = lax.axis_index("leaf")

    def device(ds, dl):
        return (lax.rem(me_s + ds + spans, spans), lax.rem(me_l + dl + leaves, leaves))

    small = [
        pltpu.make_async_copy(forces, m_forces, in_sem.at[1]),
        pltpu.make_async_copy(dest, m_dest, in_sem.at[2]),
        pltpu.make_async_copy(cells, m_cells, in_sem.at[3]),
    ]
    for copy in small:
        copy.start()
    load = pltpu.make_async_copy(pop, f, in_sem.at[0])
    load.start()

    barrier = pltpu.get_barrier_semaphore()
    greeted = [(0, k) for k in range(1, leaves)]
    greeted += [(ds, dl) for ds in (1, -1) for dl in (0, 1, -1)]
    for ds, dl in greeted:
        pl.semaphore_signal(barrier, inc=1, device_id=device(ds, dl), device_id_type=MESH)

    for k in range(27):
        power = parts(k)
        scale = 0.5 ** sum(1 for p in power if p)
        third = (1.0 / 3.0) ** sum(1 for p in power if p == 2)
        rate = rates[k]
        coef[0, k] = jnp.full((8, 128), (1.0 - rate) * scale, F32)
        coef[1, k] = jnp.full((8, 128), rate * (scale * third), F32)

    for copy in small:
        copy.wait()
    for t in range(2):
        own_dest = m_dest[t]
        own_cells = m_cells[t : t + 1, :].astype(F32)
        own_force = m_forces[:, t, :]
        for k in range(leaves):
            chosen = own_dest == device(0, k)[1]
            masked = jnp.where(chosen, own_force, 0.0)
            target = m_recv if k == 0 else m_send
            target[t, k, 0:3, :] = masked
            target[t, k, 3:4, :] = own_cells
    pl.semaphore_wait(barrier, len(greeted))

    def marker_copy(t, k):
        return pltpu.make_async_remote_copy(
            src_ref=m_send.at[t, k], dst_ref=m_recv.at[t, k],
            send_sem=ms_sem.at[t, k], recv_sem=mr_sem.at[t, k],
            device_id=device(0, k), device_id_type=MESH,
        )

    for t in range(2):
        for k in range(1, leaves):
            marker_copy(t, k).start()

    def keep(k):
        return coef[0, k]

    def pull(k):
        return coef[1, k]

    load.wait()

    def relax_plane(x, carry):
        n = relax(forward([f[q, x] for q in range(27)]), keep, pull)
        for k in range(27):
            f[k, x] = n[k]
        return carry

    lax.fori_loop(0, wx, relax_plane, 0)

    def deposit(t):
        def spread(s):
            cell = m_recv[t, s, 3:4, :].astype(jnp.int32)
            row = (cell >> 7) & 63
            column = ((cell >> 13) << 7) + (cell & 127)
            lanes = pl.ds(pl.multiple_of(s * count, 128), count)
            is_column = lax.broadcasted_iota(jnp.int32, (256, count), 0) == column
            hot_b[:, lanes] = jnp.where(is_column, 1.0, 0.0).astype(BF16)
            is_row = lax.broadcasted_iota(jnp.int32, (64, count), 0) == row
            for d in range(3):
                amount = m_recv[t, s, d : d + 1, :]
                high = amount.astype(BF16).astype(F32)
                low = amount - high
                hot_a[64 * d : 64 * d + 64, lanes] = jnp.where(is_row, high, 0.0).astype(BF16)
                hot_a[192 + 64 * d : 256 + 64 * d, lanes] = jnp.where(is_row, low, 0.0).astype(BF16)

        spread(0)

        def arrived(s, carry):
            marker_copy(t, s).wait_recv()
            spread(s)
            return carry

        lax.fori_loop(1, leaves, arrived, 0)
        both = lax.dot_general(
            hot_a[...], hot_b[...], (((1,), (1,)), ((), ())), preferred_element_type=F32
        )
        total = both[0:192] + both[192:384]
        for d in range(3):
            for side in range(2):
                block = total[64 * d : 64 * d + 64, 128 * side : 128 * side + 128]
                force[d, 8 * side : 8 * side + 8] = block.reshape(8, 8, 128)

    def put(t, post, x, n):
        n = add_force(n, [force[d, x] for d in range(3)])
        values = backward(n)
        for q in range(27):
            _, cy, cz = parts(q)
            v = values[q]
            if cy != 1:
                v = pltpu.roll(v, 1 if cy == 2 else 127, axis=1)
            if cz != 1:
                v = pltpu.roll(v, 1 if cz == 2 else 7, axis=0)
            post[q, x + 1] = v
            if cz == 2:
                send_p[t, q // 3, x] = v[0:1]
            if cz == 0:
                send_m[t, q // 3, x] = v[7:8]

    def halo(t, post):
        low, high = zlo.at[t], zhi.at[t]
        up, down = send_p.at[t], send_m.at[t]
        last = wx - 1
        plan = [
            (post.at[18:27, wx], post.at[18:27, 0], (1, 0)),
            (post.at[0:9, 1], post.at[0:9, wx + 1], (-1, 0)),
            (up, low.at[:, 1 : wx + 1], (0, 1)),
            (down, high.at[:, 1 : wx + 1], (0, -1)),
            (up.at[6:9, last], low.at[6:9, 0], (1, 1)),
            (up.at[0:3, 0], low.at[0:3, wx + 1], (-1, 1)),
            (down.at[6:9, last], high.at[6:9, 0], (1, -1)),
            (down.at[0:3, 0], high.at[0:3, wx + 1], (-1, -1)),
        ]
        return [
            pltpu.make_async_remote_copy(
                src_ref=source, dst_ref=target,
                send_sem=hs_sem.at[t, i], recv_sem=hr_sem.at[t, i],
                device_id=device(*where), device_id_type=MESH,
            )
            for i, (source, target, where) in enumerate(plan)
        ]

    sublane = lax.broadcasted_iota(jnp.int32, (8, 128), 0)

    deposit(0)

    def put_plane(x, carry):
        put(0, pa, x, [f[k, x] for k in range(27)])
        return carry

    lax.fori_loop(0, wx, put_plane, 0)
    first = halo(0, pa)
    for copy in first:
        copy.start()
    deposit(1)
    for copy in first:
        copy.wait_recv()

    def whole_plane(x, carry):
        values = []
        for q in range(27):
            cx, _, cz = parts(q)
            at = x + (2 - cx)
            v = pa[q, at]
            if cz == 2:
                v = jnp.where(sublane == 0, zlo[0, q // 3, at], v)
            if cz == 0:
                v = jnp.where(sublane == 7, zhi[0, q // 3, at], v)
            values.append(v)
        put(1, pb, x, relax(forward(values), keep, pull))
        return carry

    lax.fori_loop(0, wx, whole_plane, 0)
    second = halo(1, pb)
    for copy in second:
        copy.start()
    for copy in second:
        copy.wait_recv()
    for copy in second:
        copy.wait_send()

    def close_plane(x, carry):
        for q in range(27):
            cx, _, cz = parts(q)
            at = x + (2 - cx)
            if cz == 2:
                pb[q, at, 0:1] = zlo[1, q // 3, at]
            if cz == 0:
                pb[q, at, 7:8] = zhi[1, q // 3, at]
        return carry

    lax.fori_loop(0, wx, close_plane, 0)
    stores = [
        pltpu.make_async_copy(
            pb.at[9 * c : 9 * c + 9, 2 - c : 2 - c + wx], out.at[9 * c : 9 * c + 9], out_sem.at[c]
        )
        for c in range(3)
    ]
    for copy in stores:
        copy.start()
    for copy in first:
        copy.wait_send()
    for t in range(2):
        for k in range(1, leaves):
            marker_copy(t, k).wait_send()
    for copy in stores:
        copy.wait()


def body(spans, leaves, populations, relax_rates, marker_forces, marker_dest, marker_cells):
    steps, _, count = marker_forces.shape
    wx = populations.shape[1]
    anywhere = pl.BlockSpec(memory_space=pl.ANY)
    vmem = pltpu.VMEM
    dma = pltpu.SemaphoreType.DMA
    return pl.pallas_call(
        functools.partial(kernel, spans, leaves),
        out_shape=jax.ShapeDtypeStruct(populations.shape, F32),
        in_specs=[anywhere, pl.BlockSpec(memory_space=pltpu.SMEM), anywhere, anywhere, anywhere],
        out_specs=anywhere,
        scratch_shapes=[
            vmem(populations.shape, F32),
            vmem((27, wx + 2, 8, 128), F32),
            vmem((27, wx + 2, 8, 128), F32),
            vmem((2, 27, 8, 128), F32),
            vmem((3, wx, 8, 128), F32),
            vmem((384, leaves * count), BF16),
            vmem((256, leaves * count), BF16),
            vmem((3, steps, count), F32),
            vmem((steps, 1, count), jnp.int32),
            vmem((steps, count), jnp.int32),
            vmem((steps, leaves, 4, count), F32),
            vmem((steps, leaves, 4, count), F32),
            vmem((steps, 9, wx, 1, 128), F32),
            vmem((steps, 9, wx, 1, 128), F32),
            vmem((steps, 9, wx + 2, 1, 128), F32),
            vmem((steps, 9, wx + 2, 1, 128), F32),
            dma((4,)),
            dma((3,)),
            dma((steps, leaves)),
            dma((steps, leaves)),
            dma((steps, 8)),
            dma((steps, 8)),
        ],
        compiler_params=pltpu.CompilerParams(
            collective_id=0, has_side_effects=True, vmem_limit_bytes=56 * 1024 * 1024
        ),
        cost_estimate=pl.CostEstimate(
            flops=700 * 2 * populations.size // 27, bytes_accessed=8 * populations.size,
            transcendentals=0,
        ),
    )(
        populations, relax_rates, marker_forces.transpose(1, 0, 2),
        marker_dest.transpose(0, 2, 1), marker_cells,
    )


def solution(mesh):
    spans, leaves = mesh.shape["span"], mesh.shape["leaf"]
    placed = (
        P(None, "span", "leaf", None),
        P(),
        P(None, None, ("span", "leaf")),
        P(None, ("span", "leaf"), None),
        P(None, ("span", "leaf")),
    )
    return jax.shard_map(
        functools.partial(body, spans, leaves),
        mesh=mesh, in_specs=placed, out_specs=P(None, "span", "leaf", None), check_vma=False,
    )
```

time: 135 us -> 31.1 us (0.23)
  blocking collectives: 56.1 us -> 0 us
  matrix products: 28.3 us -> 0 us
  Pallas kernels: 0 us -> 28 us
  waiting for transfers between devices: 16 us -> 0 us
  local copies, waits for them, and re-layouts: 16.6 us -> 2.87 us
  starting transfers between devices: 9.54 us -> 0 us
  other arithmetic: 7.11 us -> 0 us
    all_gather x4 -> x0, blocking collectives: 56.1 us -> none  [the longest x2 29.4 us: deposit_forces(): lax.all_gather(jnp.stack([destinations, cell_ids]), 'leaf', axis=1, tiled...]
    dot_general x11 -> x0, matrix products: 28.3 us -> none  [the longest x2 7.4 us: collide(): moments = jnp.dot(forward, populations - equilibrium, precision=highest)]
    pallas_call x0 -> x1, Pallas kernels: none -> 28 us  [body(): pl.pallas_call(functools.partial(kernel, spans, leaves), out_shape=jax.Sh...]
    ppermute x8 -> x0, waiting for transfers between devices: 16 us -> none  [the longest x4 10.9 us: padded_2(): lax.ppermute(lax.slice_in_dim(block, 0, width, axis=dim), axis, backward)]
    ppermute x8 -> x0, starting transfers between devices: 9.54 us -> none  [the longest x4 7.36 us: padded_2(): lax.ppermute(lax.slice_in_dim(block, 0, width, axis=dim), axis, backward)]
    slice x44 -> x0, local copies, waits for them, and re-layouts: 5.39 us -> none  [the longest x36 2.93 us: stream_local(): moved.append(jnp.roll(section, shift_y, axis=2))]
    another operation x2 -> x0, local copies, waits for them, and re-layouts: 5.12 us -> none  [the longest x1 4.29 us: stream_local(): return jnp.stack(moved)]
    reduce_sum x3 -> x0, other arithmetic: 2.73 us -> none  [the longest x1 1.38 us: collide(): square = jnp.sum(velocity_field * velocity_field, axis=0)]
  transfers between devices with their start and end apart: 8 -> 0, of which waited for: 6 -> 0; matrix products, arithmetic and copies ran while one was open for 7% -> 0% of each run, Pallas kernels for 0% -> 0%
where the time goes in v1:
time: 31.1 us; the launch traced here: 30.9 us
  Pallas kernels  28 us (90%)
  local copies, waits for them, and re-layouts  2.87 us (9%)
    pallas_call x1, Pallas kernels, body(): pl.pallas_call(functools.partial(kernel, spans, leaves), out_shape=jax.Sh...  28 us
    unnamed x1, local copies, waits for them, and re-layouts  2.87 us

profile of v1, /device:TPU:0, one launch (start us, length us, event | category | flops | bytes accessed | tf_op | source)
XLA Modules:
  0.0 30.9 jit_solution(7480968288627119339)
XLA Ops:
  0.0 28.0 %shard_map.55 = f32[27,16,8,128]{3,2,1,0:T(8,128)} custom-call(f32[27,16,8,128]{3,2,1,0:T(8,128)} %pop.1, f32[27]{0:T(128)} %rates.1, f32[3,2,384]{2,1,0:T(2,128)} %bitcast.2, s32[2,1,384]{2,1,0:T(1,128)} %bitcast.3, s32[2,384]{1,0:T(2,128)} %cells.1), custom_call_target="tpu_custom_call" | custom-call | flops 22937600 | bytes 3538944 | tf_op jit(solution)/shard_map/pallas_call | solution.py:307
  28.0 2.9 %copy.7 = f32[27,16,8,128]{3,2,1,0:T(8,128)} copy(f32[27,16,8,128]{3,2,1,0:T(8,128)} %shard_map.55) | data formatting | bytes 3538944

commit v2 on v1

--- a/solution.py
+++ b/solution.py
@@ -84,7 +84,7 @@
     f, pa, pb, coef, force, hot_a, hot_b,
     m_forces, m_dest, m_cells, m_send, m_recv,
     send_p, send_m, zlo, zhi,
-    in_sem, out_sem, ms_sem, mr_sem, hs_sem, hr_sem,
+    in_sem, ms_sem, mr_sem, hs_sem, hr_sem,
 ):
     wx = pop.shape[1]
     count = cells.shape[1]
@@ -274,28 +274,20 @@
         for q in range(27):
             cx, _, cz = parts(q)
             at = x + (2 - cx)
+            v = pb[q, at]
             if cz == 2:
-                pb[q, at, 0:1] = zlo[1, q // 3, at]
+                v = jnp.where(sublane == 0, zlo[1, q // 3, at], v)
             if cz == 0:
-                pb[q, at, 7:8] = zhi[1, q // 3, at]
+                v = jnp.where(sublane == 7, zhi[1, q // 3, at], v)
+            out[q, x] = v
         return carry
 
     lax.fori_loop(0, wx, close_plane, 0)
-    stores = [
-        pltpu.make_async_copy(
-            pb.at[9 * c : 9 * c + 9, 2 - c : 2 - c + wx], out.at[9 * c : 9 * c + 9], out_sem.at[c]
-        )
-        for c in range(3)
-    ]
-    for copy in stores:
-        copy.start()
     for copy in first:
         copy.wait_send()
     for t in range(2):
         for k in range(1, leaves):
             marker_copy(t, k).wait_send()
-    for copy in stores:
-        copy.wait()
 
 
 def body(spans, leaves, populations, relax_rates, marker_forces, marker_dest, marker_cells):
@@ -306,9 +298,9 @@
     dma = pltpu.SemaphoreType.DMA
     return pl.pallas_call(
         functools.partial(kernel, spans, leaves),
-        out_shape=jax.ShapeDtypeStruct(populations.shape, F32),
+        out_shape=vmem(populations.shape, F32),
         in_specs=[anywhere, pl.BlockSpec(memory_space=pltpu.SMEM), anywhere, anywhere, anywhere],
-        out_specs=anywhere,
+        out_specs=pl.BlockSpec(memory_space=vmem),
         scratch_shapes=[
             vmem(populations.shape, F32),
             vmem((27, wx + 2, 8, 128), F32),
@@ -327,14 +319,13 @@
             vmem((steps, 9, wx + 2, 1, 128), F32),
             vmem((steps, 9, wx + 2, 1, 128), F32),
             dma((4,)),
-            dma((3,)),
             dma((steps, leaves)),
             dma((steps, leaves)),
             dma((steps, 8)),
             dma((steps, 8)),
         ],
         compiler_params=pltpu.CompilerParams(
-            collective_id=0, has_side_effects=True, vmem_limit_bytes=56 * 1024 * 1024
+            collective_id=0, has_side_effects=True, vmem_limit_bytes=60 * 1024 * 1024
         ),
         cost_estimate=pl.CostEstimate(
             flops=700 * 2 * populations.size // 27, bytes_accessed=8 * populations.size,

time: 31.1 us -> 28.3 us (0.910)
  local copies, waits for them, and re-layouts: 2.87 us -> 1.21 us
  Pallas kernels: 28 us -> 26.9 us
    unnamed x1, local copies, waits for them, and re-layouts: 2.87 us -> 1.21 us
    pallas_call x1, Pallas kernels: 28 us -> 26.9 us  [body(): pl.pallas_call(functools.partial(kernel, spans, leaves), out_shape=vmem(p...]
where the time goes in v2:
time: 28.3 us; the launch traced here: 28.1 us
  Pallas kernels  26.9 us (95%)
  local copies, waits for them, and re-layouts  1.21 us (4%)
    pallas_call x1, Pallas kernels, body(): pl.pallas_call(functools.partial(kernel, spans, leaves), out_shape=vmem(p...  26.9 us
    unnamed x1, local copies, waits for them, and re-layouts  1.21 us

profile of v2, /device:TPU:0, one launch (start us, length us, event | category | flops | bytes accessed | tf_op | source)
XLA Modules:
  0.0 28.1 jit_solution(10039011600448972659)
XLA Ops:
  0.0 26.9 %shard_map.55 = f32[27,16,8,128]{3,2,1,0:T(8,128)S(1)} custom-call(f32[27,16,8,128]{3,2,1,0:T(8,128)} %pop.1, f32[27]{0:T(128)} %rates.1, f32[3,2,384]{2,1,0:T(2,128)} %bitcast.2, s32[2,1,384]{2,1,0:T(1,128)} %bitcast.3, s32[2,384]{1,0:T(2,128)} %cells.1), custom_call_target="tpu_custom_call" | custom-call | flops 22937600 | bytes 3538944 | tf_op jit(solution)/shard_map/pallas_call | solution.py:299
  26.9 1.2 %copy.7 = f32[27,16,8,128]{3,2,1,0:T(8,128)} copy(f32[27,16,8,128]{3,2,1,0:T(8,128)S(1)} %shard_map.55) | data formatting | bytes 3538944

commit v3 on v2

--- a/solution.py
+++ b/solution.py
@@ -157,23 +157,36 @@
             f[k, x] = n[k]
         return carry
 
-    lax.fori_loop(0, wx, relax_plane, 0)
+    lax.fori_loop(0, wx, relax_plane, 0, unroll=2)
+
+    def tile(v):
+        return jnp.broadcast_to(v.astype(F32), (16, count)).astype(BF16)
+
+    one = jnp.ones((16, count), BF16)
+    zero = jnp.zeros((16, count), BF16)
+    counted = [
+        (lax.broadcasted_iota(jnp.int32, (16, count), 0) + 16 * g).astype(F32).astype(BF16)
+        for g in range(16)
+    ]
 
     def deposit(t):
         def spread(s):
             cell = m_recv[t, s, 3:4, :].astype(jnp.int32)
-            row = (cell >> 7) & 63
-            column = ((cell >> 13) << 7) + (cell & 127)
+            row = tile((cell >> 7) & 63)
+            column = tile(((cell >> 13) << 7) + (cell & 127))
             lanes = pl.ds(pl.multiple_of(s * count, 128), count)
-            is_column = lax.broadcasted_iota(jnp.int32, (256, count), 0) == column
-            hot_b[:, lanes] = jnp.where(is_column, 1.0, 0.0).astype(BF16)
-            is_row = lax.broadcasted_iota(jnp.int32, (64, count), 0) == row
+            for g in range(16):
+                hot_b[16 * g : 16 * g + 16, lanes] = jnp.where(counted[g] == column, one, zero)
+            halves = []
             for d in range(3):
                 amount = m_recv[t, s, d : d + 1, :]
                 high = amount.astype(BF16).astype(F32)
-                low = amount - high
-                hot_a[64 * d : 64 * d + 64, lanes] = jnp.where(is_row, high, 0.0).astype(BF16)
-                hot_a[192 + 64 * d : 256 + 64 * d, lanes] = jnp.where(is_row, low, 0.0).astype(BF16)
+                halves.append((64 * d, tile(high)))
+                halves.append((64 * d + 192, tile(amount - high)))
+            for g in range(4):
+                is_row = counted[g] == row
+                for start, half in halves:
+                    hot_a[start + 16 * g : start + 16 * g + 16, lanes] = jnp.where(is_row, half, zero)
 
         spread(0)
 
@@ -239,7 +252,7 @@
         put(0, pa, x, [f[k, x] for k in range(27)])
         return carry
 
-    lax.fori_loop(0, wx, put_plane, 0)
+    lax.fori_loop(0, wx, put_plane, 0, unroll=2)
     first = halo(0, pa)
     for copy in first:
         copy.start()
@@ -261,7 +274,7 @@
         put(1, pb, x, relax(forward(values), keep, pull))
         return carry
 
-    lax.fori_loop(0, wx, whole_plane, 0)
+    lax.fori_loop(0, wx, whole_plane, 0, unroll=2)
     second = halo(1, pb)
     for copy in second:
         copy.start()
@@ -282,7 +295,7 @@
             out[q, x] = v
         return carry
 
-    lax.fori_loop(0, wx, close_plane, 0)
+    lax.fori_loop(0, wx, close_plane, 0, unroll=2)
     for copy in first:
         copy.wait_send()
     for t in range(2):

time: 28.3 us -> 26.9 us (0.951)
  Pallas kernels: 26.9 us -> 25.5 us
    pallas_call x1, Pallas kernels: 26.9 us -> 25.5 us  [body(): pl.pallas_call(functools.partial(kernel, spans, leaves), out_shape=vmem(p...]
where the time goes in v3:
time: 26.9 us; the launch traced here: 26.7 us
  Pallas kernels  25.5 us (95%)
  local copies, waits for them, and re-layouts  1.21 us (4%)
    pallas_call x1, Pallas kernels, body(): pl.pallas_call(functools.partial(kernel, spans, leaves), out_shape=vmem(p...  25.5 us
    unnamed x1, local copies, waits for them, and re-layouts  1.21 us

profile of v3, /device:TPU:0, one launch (start us, length us, event | category | flops | bytes accessed | tf_op | source)
XLA Modules:
  0.0 26.7 jit_solution(11722292670394462841)
XLA Ops:
  0.0 25.5 %shard_map.55 = f32[27,16,8,128]{3,2,1,0:T(8,128)S(1)} custom-call(f32[27,16,8,128]{3,2,1,0:T(8,128)} %pop.1, f32[27]{0:T(128)} %rates.1, f32[3,2,384]{2,1,0:T(2,128)} %bitcast.2, s32[2,1,384]{2,1,0:T(1,128)} %bitcast.3, s32[2,384]{1,0:T(2,128)} %cells.1), custom_call_target="tpu_custom_call" | custom-call | flops 22937600 | bytes 3538944 | tf_op jit(solution)/shard_map/pallas_call | solution.py:312
  25.5 1.2 %copy.7 = f32[27,16,8,128]{3,2,1,0:T(8,128)} copy(f32[27,16,8,128]{3,2,1,0:T(8,128)S(1)} %shard_map.55) | data formatting | bytes 3538944

commit v4 on v3

--- a/solution.py
+++ b/solution.py
@@ -10,6 +10,7 @@
 MESH = pl.DeviceIdType.MESH
 F32 = jnp.float32
 BF16 = jnp.bfloat16
+PIECES = 4
 
 
 def parts(index):
@@ -81,7 +82,7 @@
 def kernel(
     spans, leaves,
     pop, rates, forces, dest, cells, out,
-    f, pa, pb, coef, force, hot_a, hot_b,
+    f, pa, faces, coef, force, hot_a, hot_b,
     m_forces, m_dest, m_cells, m_send, m_recv,
     send_p, send_m, zlo, zhi,
     in_sem, ms_sem, mr_sem, hs_sem, hr_sem,
@@ -139,9 +140,8 @@
             device_id=device(0, k), device_id_type=MESH,
         )
 
-    for t in range(2):
-        for k in range(1, leaves):
-            marker_copy(t, k).start()
+    for k in range(1, leaves):
+        marker_copy(0, k).start()
 
     def keep(k):
         return coef[0, k]
@@ -158,6 +158,8 @@
         return carry
 
     lax.fori_loop(0, wx, relax_plane, 0, unroll=2)
+    for k in range(1, leaves):
+        marker_copy(1, k).start()
 
     def tile(v):
         return jnp.broadcast_to(v.astype(F32), (16, count)).astype(BF16)
@@ -205,36 +207,53 @@
                 block = total[64 * d : 64 * d + 64, 128 * side : 128 * side + 128]
                 force[d, 8 * side : 8 * side + 8] = block.reshape(8, 8, 128)
 
-    def put(t, post, x, n):
+    def put(t, x, n):
         n = add_force(n, [force[d, x] for d in range(3)])
         values = backward(n)
         for q in range(27):
-            _, cy, cz = parts(q)
+            cx, cy, cz = parts(q)
             v = values[q]
             if cy != 1:
                 v = pltpu.roll(v, 1 if cy == 2 else 127, axis=1)
             if cz != 1:
                 v = pltpu.roll(v, 1 if cz == 2 else 7, axis=0)
-            post[q, x + 1] = v
+            if t == 0:
+                pa[q, x + 1] = v
+            elif cx == 0 and isinstance(x, int) and x == 0:
+                faces[0, q] = v
+            elif cx == 2 and isinstance(x, int) and x == last:
+                faces[1, q - 18] = v
+            else:
+                out[q, x + (cx - 1)] = v
             if cz == 2:
                 send_p[t, q // 3, x] = v[0:1]
             if cz == 0:
                 send_m[t, q // 3, x] = v[7:8]
 
-    def halo(t, post):
+    def halo(t):
         low, high = zlo.at[t], zhi.at[t]
         up, down = send_p.at[t], send_m.at[t]
-        last = wx - 1
-        plan = [
-            (post.at[18:27, wx], post.at[18:27, 0], (1, 0)),
-            (post.at[0:9, 1], post.at[0:9, wx + 1], (-1, 0)),
-            (up, low.at[:, 1 : wx + 1], (0, 1)),
-            (down, high.at[:, 1 : wx + 1], (0, -1)),
+        if t == 0:
+            plan = [
+                (pa.at[18:27, wx], pa.at[18:27, 0], (1, 0)),
+                (pa.at[0:9, 1], pa.at[0:9, wx + 1], (-1, 0)),
+            ]
+        else:
+            plan = [
+                (faces.at[1], out.at[18:27, 0], (1, 0)),
+                (faces.at[0], out.at[0:9, last], (-1, 0)),
+            ]
+        plan += [
             (up.at[6:9, last], low.at[6:9, 0], (1, 1)),
             (up.at[0:3, 0], low.at[0:3, wx + 1], (-1, 1)),
             (down.at[6:9, last], high.at[6:9, 0], (1, -1)),
             (down.at[0:3, 0], high.at[0:3, wx + 1], (-1, -1)),
         ]
+        for c in range(PIECES):
+            at = slice(c * piece, (c + 1) * piece)
+            to = slice(c * piece + 1, (c + 1) * piece + 1)
+            plan.append((up.at[:, at], low.at[:, to], (0, 1)))
+            plan.append((down.at[:, at], high.at[:, to], (0, -1)))
         return [
             pltpu.make_async_remote_copy(
                 src_ref=source, dst_ref=target,
@@ -244,18 +263,29 @@
             for i, (source, target, where) in enumerate(plan)
         ]
 
+    def planes(plane, copies):
+        plane(0, 0)
+        plane(last, 0)
+        for copy in copies[:6]:
+            copy.start()
+        for c in range(PIECES):
+            start, stop = max(c * piece, 1), min((c + 1) * piece, last)
+            lax.fori_loop(start, stop, plane, 0, unroll=2 if (stop - start) % 2 == 0 else True)
+            for copy in copies[6 + 2 * c : 8 + 2 * c]:
+                copy.start()
+
+    last = wx - 1
+    piece = wx // PIECES
     sublane = lax.broadcasted_iota(jnp.int32, (8, 128), 0)
 
     deposit(0)
 
     def put_plane(x, carry):
-        put(0, pa, x, [f[k, x] for k in range(27)])
+        put(0, x, [f[k, x] for k in range(27)])
         return carry
 
-    lax.fori_loop(0, wx, put_plane, 0, unroll=2)
-    first = halo(0, pa)
-    for copy in first:
-        copy.start()
+    first = halo(0)
+    planes(put_plane, first)
     deposit(1)
     for copy in first:
         copy.wait_recv()
@@ -271,31 +301,27 @@
             if cz == 0:
                 v = jnp.where(sublane == 7, zhi[0, q // 3, at], v)
             values.append(v)
-        put(1, pb, x, relax(forward(values), keep, pull))
+        put(1, x, relax(forward(values), keep, pull))
         return carry
 
-    lax.fori_loop(0, wx, whole_plane, 0, unroll=2)
-    second = halo(1, pb)
-    for copy in second:
-        copy.start()
+    second = halo(1)
+    planes(whole_plane, second)
     for copy in second:
         copy.wait_recv()
-    for copy in second:
-        copy.wait_send()
 
     def close_plane(x, carry):
         for q in range(27):
             cx, _, cz = parts(q)
             at = x + (2 - cx)
-            v = pb[q, at]
             if cz == 2:
-                v = jnp.where(sublane == 0, zlo[1, q // 3, at], v)
+                out[q, x, 0:1] = zlo[1, q // 3, at]
             if cz == 0:
-                v = jnp.where(sublane == 7, zhi[1, q // 3, at], v)
-            out[q, x] = v
+                out[q, x, 7:8] = zhi[1, q // 3, at]
         return carry
 
     lax.fori_loop(0, wx, close_plane, 0, unroll=2)
+    for copy in second:
+        copy.wait_send()
     for copy in first:
         copy.wait_send()
     for t in range(2):
@@ -317,7 +343,7 @@
         scratch_shapes=[
             vmem(populations.shape, F32),
             vmem((27, wx + 2, 8, 128), F32),
-            vmem((27, wx + 2, 8, 128), F32),
+            vmem((2, 9, 8, 128), F32),
             vmem((2, 27, 8, 128), F32),
             vmem((3, wx, 8, 128), F32),
             vmem((384, leaves * count), BF16),
@@ -334,8 +360,8 @@
             dma((4,)),
             dma((steps, leaves)),
             dma((steps, leaves)),
-            dma((steps, 8)),
-            dma((steps, 8)),
+            dma((steps, 6 + 2 * PIECES)),
+            dma((steps, 6 + 2 * PIECES)),
         ],
         compiler_params=pltpu.CompilerParams(
             collective_id=0, has_side_effects=True, vmem_limit_bytes=60 * 1024 * 1024

time: 26.9 us -> 23.4 us (0.87)
  Pallas kernels: 25.5 us -> 22 us
    pallas_call x1, Pallas kernels: 25.5 us -> 22 us  [body(): pl.pallas_call(functools.partial(kernel, spans, leaves), out_shape=vmem(p...]
where the time goes in v4:
time: 23.4 us; the launch traced here: 23.2 us
  Pallas kernels  22 us (94%)
  local copies, waits for them, and re-layouts  1.21 us (5%)
    pallas_call x1, Pallas kernels, body(): pl.pallas_call(functools.partial(kernel, spans, leaves), out_shape=vmem(p...  22 us
    unnamed x1, local copies, waits for them, and re-layouts  1.21 us

profile of v4, /device:TPU:0, one launch (start us, length us, event | category | flops | bytes accessed | tf_op | source)
XLA Modules:
  0.0 23.2 jit_solution(8997086423350645606)
XLA Ops:
  0.0 22.0 %shard_map.55 = f32[27,16,8,128]{3,2,1,0:T(8,128)S(1)} custom-call(f32[27,16,8,128]{3,2,1,0:T(8,128)} %pop.1, f32[27]{0:T(128)} %rates.1, f32[3,2,384]{2,1,0:T(2,128)} %bitcast.2, s32[2,1,384]{2,1,0:T(1,128)} %bitcast.3, s32[2,384]{1,0:T(2,128)} %cells.1), custom_call_target="tpu_custom_call" | custom-call | flops 22937600 | bytes 3538944 | tf_op jit(solution)/shard_map/pallas_call | solution.py:338
  22.0 1.2 %copy.7 = f32[27,16,8,128]{3,2,1,0:T(8,128)} copy(f32[27,16,8,128]{3,2,1,0:T(8,128)S(1)} %shard_map.55) | data formatting | bytes 3538944

commit v5 on v4

--- a/solution.py
+++ b/solution.py
@@ -82,7 +82,7 @@
 def kernel(
     spans, leaves,
     pop, rates, forces, dest, cells, out,
-    f, pa, faces, coef, force, hot_a, hot_b,
+    f, pa, faces, coef, force, hot_a, hot_b, both,
     m_forces, m_dest, m_cells, m_send, m_recv,
     send_p, send_m, zlo, zhi,
     in_sem, ms_sem, mr_sem, hs_sem, hr_sem,
@@ -172,11 +172,11 @@
     ]
 
     def deposit(t):
-        def spread(s):
+        def spread(s, side):
             cell = m_recv[t, s, 3:4, :].astype(jnp.int32)
             row = tile((cell >> 7) & 63)
             column = tile(((cell >> 13) << 7) + (cell & 127))
-            lanes = pl.ds(pl.multiple_of(s * count, 128), count)
+            lanes = slice(side * count, (side + 1) * count)
             for g in range(16):
                 hot_b[16 * g : 16 * g + 16, lanes] = jnp.where(counted[g] == column, one, zero)
             halves = []
@@ -190,17 +190,21 @@
                 for start, half in halves:
                     hot_a[start + 16 * g : start + 16 * g + 16, lanes] = jnp.where(is_row, half, zero)
 
-        spread(0)
-
-        def arrived(s, carry):
-            marker_copy(t, s).wait_recv()
-            spread(s)
+        def pair(p, carry):
+            @pl.when(p > 0)
+            def _():
+                marker_copy(t, 2 * p).wait_recv()
+
+            spread(2 * p, 0)
+            marker_copy(t, 2 * p + 1).wait_recv()
+            spread(2 * p + 1, 1)
+            both[...] += lax.dot_general(
+                hot_a[...], hot_b[...], (((1,), (1,)), ((), ())), preferred_element_type=F32
+            )
             return carry
 
-        lax.fori_loop(1, leaves, arrived, 0)
-        both = lax.dot_general(
-            hot_a[...], hot_b[...], (((1,), (1,)), ((), ())), preferred_element_type=F32
-        )
+        both[...] = jnp.zeros_like(both)
+        lax.fori_loop(0, leaves // 2, pair, 0)
         total = both[0:192] + both[192:384]
         for d in range(3):
             for side in range(2):
@@ -250,8 +254,8 @@
             (down.at[0:3, 0], high.at[0:3, wx + 1], (-1, -1)),
         ]
         for c in range(PIECES):
-            at = slice(c * piece, (c + 1) * piece)
-            to = slice(c * piece + 1, (c + 1) * piece + 1)
+            start = ends[c - 1] if c else 0
+            at, to = slice(start, ends[c]), slice(start + 1, ends[c] + 1)
             plan.append((up.at[:, at], low.at[:, to], (0, 1)))
             plan.append((down.at[:, at], high.at[:, to], (0, -1)))
         return [
@@ -264,18 +268,33 @@
         ]
 
     def planes(plane, copies):
-        plane(0, 0)
-        plane(last, 0)
+        if copies is first:
+            lax.fori_loop(0, 2, lambda i, carry: plane(i * last, carry), 0)
+        else:
+            plane(0, 0)
+            plane(last, 0)
         for copy in copies[:6]:
             copy.start()
-        for c in range(PIECES):
-            start, stop = max(c * piece, 1), min((c + 1) * piece, last)
-            lax.fori_loop(start, stop, plane, 0, unroll=2 if (stop - start) % 2 == 0 else True)
-            for copy in copies[6 + 2 * c : 8 + 2 * c]:
-                copy.start()
+
+        def pair(i, carry):
+            plane(2 * i + 1, 0)
+            plane(2 * i + 2, 0)
+            for c in range(PIECES - 1):
+
+                @pl.when(2 * i + 2 == ends[c] - 1)
+                def _():
+                    for copy in copies[6 + 2 * c : 8 + 2 * c]:
+                        copy.start()
+
+            return carry
+
+        lax.fori_loop(0, wx // 2 - 1, pair, 0)
+        for copy in copies[4 + 2 * PIECES :]:
+            copy.start()
 
     last = wx - 1
     piece = wx // PIECES
+    ends = [(c + 1) * piece + 1 for c in range(PIECES - 1)] + [wx]
     sublane = lax.broadcasted_iota(jnp.int32, (8, 128), 0)
 
     deposit(0)
@@ -346,8 +365,9 @@
             vmem((2, 9, 8, 128), F32),
             vmem((2, 27, 8, 128), F32),
             vmem((3, wx, 8, 128), F32),
-            vmem((384, leaves * count), BF16),
-            vmem((256, leaves * count), BF16),
+            vmem((384, 2 * count), BF16),
+            vmem((256, 2 * count), BF16),
+            vmem((384, 256), F32),
             vmem((3, steps, count), F32),
             vmem((steps, 1, count), jnp.int32),
             vmem((steps, count), jnp.int32),

time: 23.4 us -> 23.2 us (level)
  no operation moved by 1% of the time
where the time goes in v5:
time: 23.2 us; the launch traced here: 23 us
  Pallas kernels  21.8 us (94%)
  local copies, waits for them, and re-layouts  1.21 us (5%)
    pallas_call x1, Pallas kernels, body(): pl.pallas_call(functools.partial(kernel, spans, leaves), out_shape=vmem(p...  21.8 us
    unnamed x1, local copies, waits for them, and re-layouts  1.21 us

profile of v5, /device:TPU:0, one launch (start us, length us, event | category | flops | bytes accessed | tf_op | source)
XLA Modules:
  0.0 23.0 jit_solution(94621172341073926)
XLA Ops:
  0.0 21.8 %shard_map.55 = f32[27,16,8,128]{3,2,1,0:T(8,128)S(1)} custom-call(f32[27,16,8,128]{3,2,1,0:T(8,128)} %pop.1, f32[27]{0:T(128)} %rates.1, f32[3,2,384]{2,1,0:T(2,128)} %bitcast.2, s32[2,1,384]{2,1,0:T(1,128)} %bitcast.3, s32[2,384]{1,0:T(2,128)} %cells.1), custom_call_target="tpu_custom_call" | custom-call | flops 22937600 | bytes 3538944 | tf_op jit(solution)/shard_map/pallas_call | solution.py:357
  21.8 1.2 %copy.7 = f32[27,16,8,128]{3,2,1,0:T(8,128)} copy(f32[27,16,8,128]{3,2,1,0:T(8,128)S(1)} %shard_map.55) | data formatting | bytes 3538944

commit v6 on v5

--- a/solution.py
+++ b/solution.py
@@ -107,7 +107,7 @@
 
     barrier = pltpu.get_barrier_semaphore()
     greeted = [(0, k) for k in range(1, leaves)]
-    greeted += [(ds, dl) for ds in (1, -1) for dl in (0, 1, -1)]
+    greeted += [(1, 0), (-1, 0)]
     for ds, dl in greeted:
         pl.semaphore_signal(barrier, inc=1, device_id=device(ds, dl), device_id_type=MESH)
 

time: 23.2 us -> 23.2 us (level)
  no operation moved by 1% of the time
where the time goes in v6:
time: 23.2 us; the launch traced here: 23 us
  Pallas kernels  21.8 us (94%)
  local copies, waits for them, and re-layouts  1.21 us (5%)
    pallas_call x1, Pallas kernels, body(): pl.pallas_call(functools.partial(kernel, spans, leaves), out_shape=vmem(p...  21.8 us
    unnamed x1, local copies, waits for them, and re-layouts  1.21 us

profile of v6, /device:TPU:0, one launch (start us, length us, event | category | flops | bytes accessed | tf_op | source)
XLA Modules:
  0.0 23.0 jit_solution(16758118819914251216)
XLA Ops:
  0.0 21.8 %shard_map.55 = f32[27,16,8,128]{3,2,1,0:T(8,128)S(1)} custom-call(f32[27,16,8,128]{3,2,1,0:T(8,128)} %pop.1, f32[27]{0:T(128)} %rates.1, f32[3,2,384]{2,1,0:T(2,128)} %bitcast.2, s32[2,1,384]{2,1,0:T(1,128)} %bitcast.3, s32[2,384]{1,0:T(2,128)} %cells.1), custom_call_target="tpu_custom_call" | custom-call | flops 22937600 | bytes 3538944 | tf_op jit(solution)/shard_map/pallas_call | solution.py:357
  21.8 1.2 %copy.7 = f32[27,16,8,128]{3,2,1,0:T(8,128)} copy(f32[27,16,8,128]{3,2,1,0:T(8,128)S(1)} %shard_map.55) | data formatting | bytes 3538944

commit v7 on v6

--- a/solution.py
+++ b/solution.py
@@ -81,10 +81,10 @@
 
 def kernel(
     spans, leaves,
-    pop, rates, forces, dest, cells, out,
+    pop, rates, forces, dest, cells, out, zlo, zhi,
     f, pa, faces, coef, force, hot_a, hot_b, both,
     m_forces, m_dest, m_cells, m_send, m_recv,
-    send_p, send_m, zlo, zhi,
+    send_p, send_m,
     in_sem, ms_sem, mr_sem, hs_sem, hr_sem,
 ):
     wx = pop.shape[1]
@@ -328,17 +328,6 @@
     for copy in second:
         copy.wait_recv()
 
-    def close_plane(x, carry):
-        for q in range(27):
-            cx, _, cz = parts(q)
-            at = x + (2 - cx)
-            if cz == 2:
-                out[q, x, 0:1] = zlo[1, q // 3, at]
-            if cz == 0:
-                out[q, x, 7:8] = zhi[1, q // 3, at]
-        return carry
-
-    lax.fori_loop(0, wx, close_plane, 0, unroll=2)
     for copy in second:
         copy.wait_send()
     for copy in first:
@@ -348,17 +337,41 @@
             marker_copy(t, k).wait_send()
 
 
+def close_kernel(inner, low, high, out, whole, sem):
+    wx = inner.shape[1]
+    sublane = lax.broadcasted_iota(jnp.int32, (8, 128), 0)
+
+    def store(g):
+        return pltpu.make_async_copy(
+            whole.at[pl.ds(3 * g, 3)], out.at[pl.ds(3 * g, 3)], sem.at[g]
+        )
+
+    def group(g, carry):
+        shift = 2 - g // 3
+        for x in range(wx):
+            at = x + shift
+            whole[3 * g, x] = jnp.where(sublane == 7, high[1, g, at], inner[3 * g, x])
+            whole[3 * g + 1, x] = inner[3 * g + 1, x]
+            whole[3 * g + 2, x] = jnp.where(sublane == 0, low[1, g, at], inner[3 * g + 2, x])
+        store(g).start()
+        return carry
+
+    lax.fori_loop(0, 9, group, 0)
+    for g in range(9):
+        store(g).wait()
+
+
 def body(spans, leaves, populations, relax_rates, marker_forces, marker_dest, marker_cells):
     steps, _, count = marker_forces.shape
     wx = populations.shape[1]
     anywhere = pl.BlockSpec(memory_space=pl.ANY)
     vmem = pltpu.VMEM
     dma = pltpu.SemaphoreType.DMA
-    return pl.pallas_call(
+    inner, low, high = pl.pallas_call(
         functools.partial(kernel, spans, leaves),
-        out_shape=vmem(populations.shape, F32),
+        out_shape=[vmem(populations.shape, F32)] + [vmem((steps, 9, wx + 2, 1, 128), F32)] * 2,
         in_specs=[anywhere, pl.BlockSpec(memory_space=pltpu.SMEM), anywhere, anywhere, anywhere],
-        out_specs=pl.BlockSpec(memory_space=vmem),
+        out_specs=[pl.BlockSpec(memory_space=vmem)] * 3,
         scratch_shapes=[
             vmem(populations.shape, F32),
             vmem((27, wx + 2, 8, 128), F32),
@@ -375,8 +388,6 @@
             vmem((steps, leaves, 4, count), F32),
             vmem((steps, 9, wx, 1, 128), F32),
             vmem((steps, 9, wx, 1, 128), F32),
-            vmem((steps, 9, wx + 2, 1, 128), F32),
-            vmem((steps, 9, wx + 2, 1, 128), F32),
             dma((4,)),
             dma((steps, leaves)),
             dma((steps, leaves)),
@@ -394,6 +405,17 @@
         populations, relax_rates, marker_forces.transpose(1, 0, 2),
         marker_dest.transpose(0, 2, 1), marker_cells,
     )
+    return pl.pallas_call(
+        close_kernel,
+        out_shape=jax.ShapeDtypeStruct(populations.shape, F32),
+        in_specs=[pl.BlockSpec(memory_space=vmem)] * 3,
+        out_specs=anywhere,
+        scratch_shapes=[vmem(populations.shape, F32), dma((9,))],
+        compiler_params=pltpu.CompilerParams(vmem_limit_bytes=16 * 1024 * 1024),
+        cost_estimate=pl.CostEstimate(
+            flops=populations.size, bytes_accessed=4 * populations.size, transcendentals=0
+        ),
+    )(inner, low, high)
 
 
 def solution(mesh):

time: 23.2 us -> 23.2 us (level)
  local copies, waits for them, and re-layouts: 1.21 us -> 0 us
  Pallas kernels: 21.8 us -> 22.9 us
    unnamed x1 -> x0, local copies, waits for them, and re-layouts: 1.21 us -> none
    pallas_call x1 -> x2, Pallas kernels: 21.8 us -> 22.9 us  [the longest x1 21.6 us: body(): pl.pallas_call(functools.partial(kernel, spans, leaves), out_shape=[vmem(...]
where the time goes in v7:
time: 23.2 us; the launch traced here: 22.9 us
  Pallas kernels  22.9 us (99%)
    pallas_call x1, Pallas kernels, body(): pl.pallas_call(functools.partial(kernel, spans, leaves), out_shape=[vmem(...  21.6 us
    pallas_call x1, Pallas kernels, body(): pl.pallas_call(close_kernel, out_shape=jax.ShapeDtypeStruct(populations.s...  1.3 us

profile of v7, /device:TPU:0, one launch (start us, length us, event | category | flops | bytes accessed | tf_op | source)
XLA Modules:
  0.0 22.9 jit_solution(15198887048293984233)
XLA Ops:
  0.0 21.6 %shard_map.55 = (f32[27,16,8,128]{3,2,1,0:T(8,128)S(1)}, f32[2,9,18,1,128]{4,3,2,1,0:T(1,128)S(1)}, f32[2,9,18,1,128]{4,3,2,1,0:T(1,128)S(1)}) custom-call(f32[27,16,8,128]{3,2,1,0:T(8,128)} %pop.1, f32[27]{0:T(128)} %rates.1, f32[3,2,384]{2,1,0:T(2,128)} %bitcast.2, s32[2,1,384]{2,1,0:T(1,128)} %bitcast.3, s32[2,384]{1,0:T(2,128)} %cells.1), custom_call_target="tpu_custom_call" | custom-call | flops 22937600 | bytes 3538944 | tf_op jit(solution)/shard_map/pallas_call | solution.py:370
  21.6 1.3 %shard_map.56 = f32[27,16,8,128]{3,2,1,0:T(8,128)} custom-call(f32[27,16,8,128]{3,2,1,0:T(8,128)S(1)} %get-tuple-element.8.inner, f32[2,9,18,1,128]{4,3,2,1,0:T(1,128)S(1)} %get-tuple-element.9.low, f32[2,9,18,1,128]{4,3,2,1,0:T(1,128)S(1)} %get-tuple-element.10.high), custom_call_target="tpu_custom_call" | custom-call | flops 442368 | bytes 1769472 | tf_op jit(solution)/shard_map/pallas_call | solution.py:408

commit v8 on v7

--- a/solution.py
+++ b/solution.py
@@ -172,13 +172,14 @@
     ]
 
     def deposit(t):
-        def spread(s, side):
+        def spread(s):
+            a, b, side = hot_a.at[s // 2 % 2], hot_b.at[s // 2 % 2], s % 2
             cell = m_recv[t, s, 3:4, :].astype(jnp.int32)
             row = tile((cell >> 7) & 63)
             column = tile(((cell >> 13) << 7) + (cell & 127))
             lanes = slice(side * count, (side + 1) * count)
             for g in range(16):
-                hot_b[16 * g : 16 * g + 16, lanes] = jnp.where(counted[g] == column, one, zero)
+                b[16 * g : 16 * g + 16, lanes] = jnp.where(counted[g] == column, one, zero)
             halves = []
             for d in range(3):
                 amount = m_recv[t, s, d : d + 1, :]
@@ -188,23 +189,21 @@
             for g in range(4):
                 is_row = counted[g] == row
                 for start, half in halves:
-                    hot_a[start + 16 * g : start + 16 * g + 16, lanes] = jnp.where(is_row, half, zero)
-
-        def pair(p, carry):
-            @pl.when(p > 0)
-            def _():
-                marker_copy(t, 2 * p).wait_recv()
-
-            spread(2 * p, 0)
-            marker_copy(t, 2 * p + 1).wait_recv()
-            spread(2 * p + 1, 1)
-            both[...] += lax.dot_general(
-                hot_a[...], hot_b[...], (((1,), (1,)), ((), ())), preferred_element_type=F32
+                    a[start + 16 * g : start + 16 * g + 16, lanes] = jnp.where(is_row, half, zero)
+
+        marker_copy(t, 1).wait_recv()
+        spread(0)
+        spread(1)
+        for p in range(leaves // 2):
+            ahead = [2 * p + 2, 2 * p + 3] if 2 * p + 2 < leaves else []
+            for sender in ahead:
+                marker_copy(t, sender).wait_recv()
+            product = lax.dot_general(
+                hot_a[p % 2], hot_b[p % 2], (((1,), (1,)), ((), ())), preferred_element_type=F32
             )
-            return carry
-
-        both[...] = jnp.zeros_like(both)
-        lax.fori_loop(0, leaves // 2, pair, 0)
+            both[...] = product if p == 0 else both[...] + product
+            for sender in ahead:
+                spread(sender)
         total = both[0:192] + both[192:384]
         for d in range(3):
             for side in range(2):
@@ -378,8 +377,8 @@
             vmem((2, 9, 8, 128), F32),
             vmem((2, 27, 8, 128), F32),
             vmem((3, wx, 8, 128), F32),
-            vmem((384, 2 * count), BF16),
-            vmem((256, 2 * count), BF16),
+            vmem((2, 384, 2 * count), BF16),
+            vmem((2, 256, 2 * count), BF16),
             vmem((384, 256), F32),
             vmem((3, steps, count), F32),
             vmem((steps, 1, count), jnp.int32),

time: 23.2 us -> 23.6 us (1.017)
  Pallas kernels: 22.9 us -> 23.3 us
    pallas_call x1, Pallas kernels: 21.6 us -> 22 us  [body(): pl.pallas_call(functools.partial(kernel, spans, leaves), out_shape=[vmem(...]
where the time goes in v8:
time: 23.6 us; the launch traced here: 23.4 us
  Pallas kernels  23.3 us (99%)
    pallas_call x1, Pallas kernels, body(): pl.pallas_call(functools.partial(kernel, spans, leaves), out_shape=[vmem(...  22 us
    pallas_call x1, Pallas kernels, body(): pl.pallas_call(close_kernel, out_shape=jax.ShapeDtypeStruct(populations.s...  1.3 us

profile of v8, /device:TPU:0, one launch (start us, length us, event | category | flops | bytes accessed | tf_op | source)
XLA Modules:
  0.0 23.4 jit_solution(9067399234341427198)
XLA Ops:
  0.0 22.0 %shard_map.55 = (f32[27,16,8,128]{3,2,1,0:T(8,128)S(1)}, f32[2,9,18,1,128]{4,3,2,1,0:T(1,128)S(1)}, f32[2,9,18,1,128]{4,3,2,1,0:T(1,128)S(1)}) custom-call(f32[27,16,8,128]{3,2,1,0:T(8,128)} %pop.1, f32[27]{0:T(128)} %rates.1, f32[3,2,384]{2,1,0:T(2,128)} %bitcast.2, s32[2,1,384]{2,1,0:T(1,128)} %bitcast.3, s32[2,384]{1,0:T(2,128)} %cells.1), custom_call_target="tpu_custom_call" | custom-call | flops 22937600 | bytes 3538944 | tf_op jit(solution)/shard_map/pallas_call | solution.py:369
  22.0 1.3 %shard_map.56 = f32[27,16,8,128]{3,2,1,0:T(8,128)} custom-call(f32[27,16,8,128]{3,2,1,0:T(8,128)S(1)} %get-tuple-element.8.inner, f32[2,9,18,1,128]{4,3,2,1,0:T(1,128)S(1)} %get-tuple-element.9.low, f32[2,9,18,1,128]{4,3,2,1,0:T(1,128)S(1)} %get-tuple-element.10.high), custom_call_target="tpu_custom_call" | custom-call | flops 442368 | bytes 1769472 | tf_op jit(solution)/shard_map/pallas_call | solution.py:407

commit v9 on v7

--- a/solution.py
+++ b/solution.py
@@ -10,7 +10,7 @@
 MESH = pl.DeviceIdType.MESH
 F32 = jnp.float32
 BF16 = jnp.bfloat16
-PIECES = 4
+PIECES = 7
 
 
 def parts(index):

time: 23.2 us -> 23.8 us (1.026)
  Pallas kernels: 22.9 us -> 23.6 us
    pallas_call x1, Pallas kernels: 21.6 us -> 22.3 us  [body(): pl.pallas_call(functools.partial(kernel, spans, leaves), out_shape=[vmem(...]
where the time goes in v9:
time: 23.8 us; the launch traced here: 23.6 us
  Pallas kernels  23.6 us (99%)
    pallas_call x1, Pallas kernels, body(): pl.pallas_call(functools.partial(kernel, spans, leaves), out_shape=[vmem(...  22.3 us
    pallas_call x1, Pallas kernels, body(): pl.pallas_call(close_kernel, out_shape=jax.ShapeDtypeStruct(populations.s...  1.3 us

profile of v9, /device:TPU:0, one launch (start us, length us, event | category | flops | bytes accessed | tf_op | source)
XLA Modules:
  0.0 23.6 jit_solution(861723629718199488)
XLA Ops:
  0.0 22.3 %shard_map.55 = (f32[27,16,8,128]{3,2,1,0:T(8,128)S(1)}, f32[2,9,18,1,128]{4,3,2,1,0:T(1,128)S(1)}, f32[2,9,18,1,128]{4,3,2,1,0:T(1,128)S(1)}) custom-call(f32[27,16,8,128]{3,2,1,0:T(8,128)} %pop.1, f32[27]{0:T(128)} %rates.1, f32[3,2,384]{2,1,0:T(2,128)} %bitcast.2, s32[2,1,384]{2,1,0:T(1,128)} %bitcast.3, s32[2,384]{1,0:T(2,128)} %cells.1), custom_call_target="tpu_custom_call" | custom-call | flops 22937600 | bytes 3538944 | tf_op jit(solution)/shard_map/pallas_call | solution.py:370
  22.3 1.3 %shard_map.56 = f32[27,16,8,128]{3,2,1,0:T(8,128)} custom-call(f32[27,16,8,128]{3,2,1,0:T(8,128)S(1)} %get-tuple-element.8.inner, f32[2,9,18,1,128]{4,3,2,1,0:T(1,128)S(1)} %get-tuple-element.9.low, f32[2,9,18,1,128]{4,3,2,1,0:T(1,128)S(1)} %get-tuple-element.10.high), custom_call_target="tpu_custom_call" | custom-call | flops 442368 | bytes 1769472 | tf_op jit(solution)/shard_map/pallas_call | solution.py:408

commit v10 on v7

--- a/solution.py
+++ b/solution.py
@@ -325,16 +325,15 @@
 
     second = halo(1)
     planes(whole_plane, second)
-    for copy in second:
-        copy.wait_recv()
-
-    for copy in second:
-        copy.wait_send()
     for copy in first:
         copy.wait_send()
     for t in range(2):
         for k in range(1, leaves):
             marker_copy(t, k).wait_send()
+    for copy in second:
+        copy.wait_send()
+    for copy in second:
+        copy.wait_recv()
 
 
 def close_kernel(inner, low, high, out, whole, sem):

time: 23.2 us -> 23.1 us (level)
  no operation moved by 1% of the time
where the time goes in v10:
time: 23.1 us; the launch traced here: 22.9 us
  Pallas kernels  22.9 us (99%)
    pallas_call x1, Pallas kernels, body(): pl.pallas_call(functools.partial(kernel, spans, leaves), out_shape=[vmem(...  21.6 us
    pallas_call x1, Pallas kernels, body(): pl.pallas_call(close_kernel, out_shape=jax.ShapeDtypeStruct(populations.s...  1.3 us

profile of v10, /device:TPU:0, one launch (start us, length us, event | category | flops | bytes accessed | tf_op | source)
XLA Modules:
  0.0 22.9 jit_solution(2411333688257842808)
XLA Ops:
  0.0 21.6 %shard_map.55 = (f32[27,16,8,128]{3,2,1,0:T(8,128)S(1)}, f32[2,9,18,1,128]{4,3,2,1,0:T(1,128)S(1)}, f32[2,9,18,1,128]{4,3,2,1,0:T(1,128)S(1)}) custom-call(f32[27,16,8,128]{3,2,1,0:T(8,128)} %pop.1, f32[27]{0:T(128)} %rates.1, f32[3,2,384]{2,1,0:T(2,128)} %bitcast.2, s32[2,1,384]{2,1,0:T(1,128)} %bitcast.3, s32[2,384]{1,0:T(2,128)} %cells.1), custom_call_target="tpu_custom_call" | custom-call | flops 22937600 | bytes 3538944 | tf_op jit(solution)/shard_map/pallas_call | solution.py:369
  21.6 1.3 %shard_map.56 = f32[27,16,8,128]{3,2,1,0:T(8,128)} custom-call(f32[27,16,8,128]{3,2,1,0:T(8,128)S(1)} %get-tuple-element.8.inner, f32[2,9,18,1,128]{4,3,2,1,0:T(1,128)S(1)} %get-tuple-element.9.low, f32[2,9,18,1,128]{4,3,2,1,0:T(1,128)S(1)} %get-tuple-element.10.high), custom_call_target="tpu_custom_call" | custom-call | flops 442368 | bytes 1769472 | tf_op jit(solution)/shard_map/pallas_call | solution.py:407

commit v11 on v10

--- a/solution.py
+++ b/solution.py
@@ -10,7 +10,7 @@
 MESH = pl.DeviceIdType.MESH
 F32 = jnp.float32
 BF16 = jnp.bfloat16
-PIECES = 4
+PIECES = 2
 
 
 def parts(index):

time: 23.1 us -> 23.3 us (level)
  no operation moved by 1% of the time
where the time goes in v11:
time: 23.3 us; the launch traced here: 23 us
  Pallas kernels  23 us (99%)
    pallas_call x1, Pallas kernels, body(): pl.pallas_call(functools.partial(kernel, spans, leaves), out_shape=[vmem(...  21.7 us
    pallas_call x1, Pallas kernels, body(): pl.pallas_call(close_kernel, out_shape=jax.ShapeDtypeStruct(populations.s...  1.3 us

profile of v11, /device:TPU:0, one launch (start us, length us, event | category | flops | bytes accessed | tf_op | source)
XLA Modules:
  0.0 23.0 jit_solution(9012528550355836524)
XLA Ops:
  0.0 21.7 %shard_map.55 = (f32[27,16,8,128]{3,2,1,0:T(8,128)S(1)}, f32[2,9,18,1,128]{4,3,2,1,0:T(1,128)S(1)}, f32[2,9,18,1,128]{4,3,2,1,0:T(1,128)S(1)}) custom-call(f32[27,16,8,128]{3,2,1,0:T(8,128)} %pop.1, f32[27]{0:T(128)} %rates.1, f32[3,2,384]{2,1,0:T(2,128)} %bitcast.2, s32[2,1,384]{2,1,0:T(1,128)} %bitcast.3, s32[2,384]{1,0:T(2,128)} %cells.1), custom_call_target="tpu_custom_call" | custom-call | flops 22937600 | bytes 3538944 | tf_op jit(solution)/shard_map/pallas_call | solution.py:369
  21.7 1.3 %shard_map.56 = f32[27,16,8,128]{3,2,1,0:T(8,128)} custom-call(f32[27,16,8,128]{3,2,1,0:T(8,128)S(1)} %get-tuple-element.8.inner, f32[2,9,18,1,128]{4,3,2,1,0:T(1,128)S(1)} %get-tuple-element.9.low, f32[2,9,18,1,128]{4,3,2,1,0:T(1,128)S(1)} %get-tuple-element.10.high), custom_call_target="tpu_custom_call" | custom-call | flops 442368 | bytes 1769472 | tf_op jit(solution)/shard_map/pallas_call | solution.py:407
